TPU v7x, 32 devices: a whole 2x2x4 slice. The times are simulated.
32 devices in a mesh: tensor: 4 (over z), expert: 8 (over y, x, core).
Axes of the slice: x: 2, y: 2, z: 4, core: 2. Of those that a mesh axis runs over, the one named last changes fastest.
Arguments:
- queries: bfloat16 [512, 64, 576], P('expert', 'tensor'), may hold values from -50 to 50
- latent_cache: bfloat16 [8192, 576], P('expert'), may hold values from -5 to 5
- new_latents: bfloat16 [512, 576], P('expert'), may hold values from -5 to 5
- residual: bfloat16 [512, 3584], P(('expert', 'tensor')), may hold values from -6 to 6
- w_uv: bfloat16 [32768, 128], P(('tensor', 'expert')), may hold values from -0.25 to 0.25
- w_out: bfloat16 [8192, 3584], P(('tensor', 'expert')), may hold values from -0.0625 to 0.0625
- norm_gain: float32 [3584], replicated, may hold values from 0.25 to 1.75
- expert_ids: int32 [512, 8], P('expert'), may hold values from 0 to 31, all different within a row; in each aligned block of 64 rows (0 to 63, 64 to 127, ...) at most 32 rows name the same one
- gate_weights: float32 [512, 8], P('expert'), may hold values from 0.1 to 0.6
- w_gate: bfloat16 [32, 3584, 1024], P('expert', None, 'tensor'), may hold values from -0.09375 to 0.09375
- w_up: bfloat16 [32, 3584, 1024], P('expert', None, 'tensor'), may hold values from -0.09375 to 0.09375
- w_down: bfloat16 [32, 1024, 3584], P('expert', 'tensor'), may hold values from -0.1875 to 0.1875
Outputs:
- layer_out: bfloat16 [512, 3584], P(('expert', 'tensor'))
Inputs may be any that keep to these rules, and one draw needn't show every extreme that they name: `expert_ids`: within each token group of 64 tokens no expert is chosen by more than 32 routes, some expert by exactly 32; a token names 8 different experts.
All inputs are finite; a program needn't handle non-finite values.
Results may differ from a plain program's by a relative error of at most 0.01.
Values may be sent and summed in bfloat16 or wider, within the bound.
A program may use at most 128 MiB of HBM per device.

v0:
```python
import jax
import jax.numpy as jnp
from jax import lax
from jax.sharding import PartitionSpec as P

LATENT = 512
ROPE = 64
VDIM = 128
TOP = 8


EPSILON = 1e-06


def route_slots(route_ids, experts_all):
    onehot = (route_ids[:, None] == jnp.arange(experts_all, dtype=jnp.int32)[None, :]).astype(
        jnp.int32
    )
    before = jnp.cumsum(onehot, axis=0) - onehot
    return jnp.sum(before * onehot, axis=1)


def rms_rows(rows, norm_gain):
    scale_rows = lax.rsqrt(jnp.mean(rows * rows, axis=1, keepdims=True) + EPSILON)
    return (rows * scale_rows * norm_gain).astype(jnp.bfloat16)


def expert_apply(arrived_rows, w_gate, w_up, w_down):
    gate_part = jnp.einsum(
        "secd,edf->secf", arrived_rows, w_gate, preferred_element_type=jnp.float32
    )
    up_part = jnp.einsum("secd,edf->secf", arrived_rows, w_up, preferred_element_type=jnp.float32)
    active = (jax.nn.silu(gate_part) * up_part).astype(jnp.bfloat16)
    return jnp.einsum("secf,efd->secd", active, w_down, preferred_element_type=jnp.float32).astype(
        jnp.bfloat16
    )


def send_back(outputs):
    return lax.all_to_all(outputs, "expert", split_axis=0, concat_axis=0, tiled=True)


def per_device(
    queries,
    latent_cache,
    new_latents,
    residual,
    w_uv,
    w_out,
    norm_gain,
    expert_ids,
    gate_weights,
    w_gate,
    w_up,
    w_down,
):
    group_count = lax.axis_size("expert")
    tok_rows = queries.shape[0]
    head_count = queries.shape[1]
    model_width = residual.shape[1]
    context = latent_cache.shape[0]
    uv_rows, out_rows = (
        lax.all_gather(w_uv, "expert", axis=0, tiled=True),
        lax.all_gather(w_out, "expert", axis=0, tiled=True),
    )
    key_rows = jnp.concatenate([latent_cache, new_latents], axis=0)
    scores = jnp.einsum("thc,kc->htk", queries, key_rows, preferred_element_type=jnp.float32) * (
        VDIM + ROPE
    ) ** (-0.5)
    query_pos = jnp.arange(tok_rows, dtype=jnp.int32)[:, None]
    key_pos = jnp.arange(key_rows.shape[0], dtype=jnp.int32)[None, :] - context
    scores = jnp.where((key_pos <= query_pos)[None], scores, -jnp.inf)
    row_peak = jnp.max(scores, axis=2, keepdims=True)
    exp_scores = jnp.exp(scores - row_peak)
    attn_probs = (exp_scores / jnp.sum(exp_scores, axis=2, keepdims=True)).astype(jnp.bfloat16)
    attended = jnp.einsum(
        "htk,kl->thl", attn_probs, key_rows[:, :LATENT], preferred_element_type=jnp.float32
    ).astype(jnp.bfloat16)
    head_values = jnp.einsum(
        "thl,hlv->thv",
        attended,
        uv_rows.reshape(head_count, LATENT, VDIM),
        preferred_element_type=jnp.float32,
    ).astype(jnp.bfloat16)
    partial_value = jnp.dot(
        head_values.reshape(tok_rows, head_count * VDIM),
        out_rows,
        preferred_element_type=jnp.float32,
    )
    own_hidden = lax.psum_scatter(
        partial_value.astype(jnp.bfloat16), "tensor", scatter_dimension=0, tiled=True
    ).astype(jnp.float32) + residual.astype(jnp.float32)
    normed = lax.all_gather(rms_rows(own_hidden, norm_gain), "tensor", axis=0, tiled=True)
    local_experts = w_gate.shape[0]
    experts_all = local_experts * group_count
    capacity = 2 * tok_rows * TOP // experts_all
    route_ids = expert_ids.reshape(-1)
    slot_numbers = route_slots(route_ids, experts_all)
    slot_index = route_ids * capacity + slot_numbers
    source = jnp.arange(route_ids.shape[0], dtype=jnp.int32) // TOP
    outgoing = (
        jnp.zeros((experts_all * capacity, model_width), jnp.bfloat16)
        .at[slot_index]
        .set(jnp.take(normed, source, axis=0))
    )
    outgoing = outgoing.reshape(group_count, local_experts, capacity, model_width)
    produced = expert_apply(
        lax.all_to_all(outgoing, "expert", split_axis=0, concat_axis=0, tiled=True),
        w_gate,
        w_up,
        w_down,
    )
    result = send_back(produced)
    weights_flat = gate_weights.reshape(-1)
    routed = (
        jnp.take(result.reshape(experts_all * capacity, model_width), slot_index, axis=0).astype(
            jnp.float32
        )
        * weights_flat[:, None]
    )
    mixed_sum = jnp.sum(routed.reshape(tok_rows, TOP, model_width), axis=1)
    summed = lax.psum_scatter(
        mixed_sum.astype(jnp.bfloat16), "tensor", scatter_dimension=0, tiled=True
    ).astype(jnp.float32)
    return (own_hidden + summed).astype(jnp.bfloat16)


def solution(mesh):
    placed = (
        P("expert", "tensor", None),
        P("expert", None),
        P("expert", None),
        P(("expert", "tensor"), None),
        P(("tensor", "expert"), None),
        P(("tensor", "expert"), None),
        P(),
        P("expert", None),
        P("expert", None),
        P("expert", None, "tensor"),
        P("expert", None, "tensor"),
        P("expert", "tensor", None),
    )
    return jax.shard_map(
        per_device,
        mesh=mesh,
        in_specs=placed,
        out_specs=P(("expert", "tensor"), None),
        check_vma=False,
    )
```

profile of v0, /device:TPU:0, one launch (start us, length us, event | category | flops | bytes accessed | tf_op | source)
XLA Modules:
  0.0 439.8 jit_solution(9496447256299166456)
XLA Ops:
  6.5 0.7 all-gather.3.cloned.1.call-update
  7.3 0.0 all-gather.5.cloned.1.call-start
  7.3 0.7 all-gather.5.cloned.1.call-update
  8.0 0.0 reduce-scatter.3.cloned.1.call-start
  8.1 1.0 copy.39
  9.1 0.8 copy.43
  9.9 0.1 eq.26
  10.0 1.2 reduce-window.6
  11.1 0.0 copy-done
  11.1 3.5 convolution_multiply_fusion
  14.7 0.0 copy-start.8
  14.7 2.1 copy-done.9
  16.8 1.5 exponential_reduce_fusion
  18.3 21.6 %all-gather.3.cloned.1.call-done = bf16[8192,128]{1,0:T(8,128)(2,1)} async-done(((bf16[1024,128]{1,0:T(8,128)(2,1)}), bf16[8192,128]{1,0:T(8,128)(2,1)}) %all-gather.3.cloned.1.call-update) | async-done | bytes 2097168 | tf_op jit(solution)/shard_map/all_gather | solution.py:63
  39.9 6.4 %fusion.53 = bf16[16,8,8,128]{3,2,1,0:T(8,128)(2,1)S(1)} fusion(bf16[16,512,128]{2,1,0:T(8,128)(2,1)} %bitcast.103, f32[16,64]{1,0:T(8,128)S(1)} %exponential_reduce_fusion, bf16[1024,576]{0,1:T(8,128)(2,1)S(1)} %copy-done.8, bf16[64,576]{0,1:T(8,128)(2,1)S(1)} %copy.39, f32[1088,64,16]{0,1,2:T(8,128)} %copy-done.9, pred[64,1088]{1,0:T(8,128)(4,1)S(1)} %iota_compare_fusion), kind=kOutput, calls=%fused_computation.43 | convolution fusion | flops 1282410496 | bytes 8142848 | tf_op jit(solution)/shard_map/thl,hlv->thv/dot_general | solution.py:79
  46.3 0.0 copy-start.5
  46.3 0.0 copy-start.3
  46.3 0.0 copy-start.6
  46.3 76.5 %all-gather.5.cloned.1.call-done = bf16[2048,3584]{1,0:T(8,128)(2,1)} async-done(((bf16[256,3584]{1,0:T(8,128)(2,1)}), bf16[2048,3584]{1,0:T(8,128)(2,1)}) %all-gather.5.cloned.1.call-update) | async-done | bytes 14680080 | tf_op jit(solution)/shard_map/all_gather | solution.py:64
  122.8 8.6 %convolution_convert_fusion.1 = bf16[64,3584]{1,0:T(8,128)(2,1)} fusion(bf16[2048,3584]{1,0:T(8,128)(2,1)} %all-gather.5.cloned.1.call-done, bf16[16,8,8,128]{3,2,1,0:T(8,128)(2,1)S(1)} %fusion.53), kind=kOutput, calls=%fused_computation.18 | convolution fusion | flops 939753472 | bytes 15400960 | tf_op jit(solution)/shard_map/dot_general | solution.py:85
  131.4 0.0 reduce-scatter.3.cloned.1.call-update
  131.4 0.2 slice_reduce_fusion
  131.6 0.1 reshape.166
  131.8 0.1 copy.48
  131.9 0.1 mul.72
  132.0 0.1 fusion.66
  132.1 20.6 %reduce-scatter.3.cloned.1.call-done = bf16[16,3584]{1,0:T(8,128)(2,1)} async-done(((bf16[64,3584]{1,0:T(8,128)(2,1)}), bf16[16,3584]{1,0:T(8,128)(2,1)}) %reduce-scatter.3.cloned.1.call-update) | async-done | bytes 114704 | tf_op jit(solution)/shard_map/reduce_scatter | solution.py:90
  152.7 1.0 multiply_reduce_fusion.1
  153.7 1.0 multiply_convert_fusion
  154.7 15.5 %all_gather.11 = bf16[64,3584]{1,0:T(8,128)(2,1)S(1)} all-gather(bf16[16,3584]{1,0:T(8,128)(2,1)S(1)} %multiply_convert_fusion), channel_id=1, replica_groups=mesh['tensor'=4,'expert'=8] {'tensor'}, dimensions={0}, use_global_device_ids=true | all-gather | bytes 573440 | tf_op jit(solution)/shard_map/all_gather | solution.py:93
  170.2 20.8 %scatter_custom_fusion = bf16[1024,3584]{1,0:T(8,128)(2,1)} fusion(s32[512]{0:T(512)S(1)} %bitcast.100, bf16[]{:T(256)} %constant.66.clone.1, pred[512]{0:T(512)(128)(4,1)S(1)} %compare_and_fusion.1, bf16[64,3584]{1,0:T(8,128)(2,1)S(1)} %all_gather.11, s32[1024]{0:T(1024)S(1)} %pad_clamp_fusion.1), kind=kCustom, calls=%fused_computation.22 | custom fusion | flops 1835008 | bytes 7803394 | tf_op jit(solution)/shard_map/scatter | solution.py:104
  191.0 86.5 %all_to_all.10 = bf16[8,4,32,3584]{3,2,1,0:T(8,128)(2,1)S(1)} all-to-all(bf16[8,4,32,3584]{3,2,1,0:T(8,128)(2,1)} %bitcast.98), channel_id=1, replica_groups=mesh['tensor'=4,'expert'=8] {'expert'}, dimensions={0} | all-to-all | bytes 14680064 | tf_op jit(solution)/shard_map/all_to_all | solution.py:108
  277.5 3.0 copy-done.2
  280.5 5.1 %fusion.19 = f32[8,4,32,256]{3,2,0,1:T(8,128)S(1)} fusion(bf16[4,3584,256]{2,1,0:T(8,128)(2,1)} %param.21, bf16[8,4,32,3584]{3,2,1,0:T(8,128)(2,1)S(1)} %all_to_all.10), kind=kOutput, calls=%fused_computation.31 | convolution fusion | flops 1879048192 | bytes 15728640 | tf_op jit(solution)/shard_map/secd,edf->secf/dot_general | solution.py:29
  285.7 14.3 %fusion.6 = bf16[8,4,32,3584]{3,2,0,1:T(8,128)(2,1)} fusion(bf16[4,256,3584]{2,1,0:T(8,128)(2,1)} %param.23, bf16[4,3584,256]{2,1,0:T(8,128)(2,1)} %param.22, bf16[8,4,32,3584]{3,2,1,0:T(8,128)(2,1)} %copy-done.2, f32[8,4,32,256]{3,2,0,1:T(8,128)S(1)} %fusion.19), kind=kOutput, calls=%fused_computation.11 | convolution fusion | flops 3763339264 | bytes 30408704 | tf_op jit(solution)/shard_map/secf,efd->secd/dot_general | solution.py:34
  300.0 6.9 %copy.51 = bf16[8,4,32,3584]{3,2,1,0:T(8,128)(2,1)} copy(bf16[8,4,32,3584]{3,2,0,1:T(8,128)(2,1)} %fusion.6) | data formatting | bytes 14680064 | tf_op jit(solution)/shard_map/convert_element_type | solution.py:34
  306.9 5.0 %all-to-all-start.1 = ((bf16[8,4,32,3584]{3,2,1,0:T(8,128)(2,1)}), bf16[8,4,32,3584]{3,2,1,0:T(8,128)(2,1)}, u32[]{:S(2)}, u32[]{:S(2)}) async-start(bf16[8,4,32,3584]{3,2,1,0:T(8,128)(2,1)} %copy.51), calls=%async_computation.2 | async-start | bytes 14680064 | tf_op jit(solution)/shard_map/all_to_all | solution.py:40
  311.9 0.3 reduce-scatter.5.cloned.1.call-start
  312.2 0.1 reduce_sum.42
  312.3 0.1 copy.46
  312.3 0.1 copy.47
  312.5 0.1 copy.52
  312.5 82.2 %all-to-all-done.1 = bf16[8,4,32,3584]{3,2,1,0:T(8,128)(2,1)} async-done(((bf16[8,4,32,3584]{3,2,1,0:T(8,128)(2,1)}), bf16[8,4,32,3584]{3,2,1,0:T(8,128)(2,1)}, u32[]{:S(2)}, u32[]{:S(2)}) %all-to-all-start.1) | async-done | bytes 7340064 | tf_op jit(solution)/shard_map/all_to_all | solution.py:40
  394.7 12.0 %gather_fusion = bf16[512,3584]{1,0:T(8,128)(2,1)} fusion(bf16[1024,3584]{1,0:T(8,128)(2,1)} %bitcast.19, s32[1024]{0:T(1024)S(1)} %pad_clamp_fusion), kind=kCustom, calls=%fused_computation.1 | custom fusion | bytes 7342080 | tf_op jit(solution)/shard_map/jit(_take)/gather | solution.py:116
  406.7 6.8 %multiply_reduce_fusion = bf16[64,3584]{1,0:T(8,128)(2,1)} fusion(bf16[512,3584]{1,0:T(8,128)(2,1)} %gather_fusion, f32[64,8]{1,0:T(8,128)S(1)} %copy.52, pred[64,8]{1,0:T(8,128)(4,1)S(1)} %copy.47), kind=kLoop, calls=%fused_computation.10 | loop fusion | flops 7110656 | bytes 4131328 | tf_op jit(solution)/shard_map/reduce_sum | solution.py:121
  413.5 0.0 reduce-scatter.5.cloned.1.call-update
  413.6 17.7 %reduce-scatter.5.cloned.1.call-done = bf16[16,3584]{1,0:T(8,128)(2,1)} async-done(((bf16[64,3584]{1,0:T(8,128)(2,1)}), bf16[16,3584]{1,0:T(8,128)(2,1)}) %reduce-scatter.5.cloned.1.call-update) | async-done | bytes 114704 | tf_op jit(solution)/shard_map/reduce_scatter | solution.py:122
  431.3 1.6 add_convert_fusion
  (27 shorter events, 0.2 us)
Async XLA Ops:
  6.5 4.6 %copy-start = (bf16[64,16,576]{2,1,0:T(8,128)(2,1)S(1)}, bf16[64,16,576]{2,1,0:T(8,128)(2,1)}, u32[]{:S(2)}) copy-start(bf16[64,16,576]{2,1,0:T(8,128)(2,1)} %param.12) | copy-start | bytes 3538948
  6.5 33.4 %all-gather.3.cloned.1.call-start = ((), (), s32[]{:S(2)}) async-start(), calls=%async_computation.4 | async-start | bytes 2359296 | tf_op jit(solution)/shard_map/all_gather | solution.py:63
  7.3 115.5 %all-gather.5.cloned.1.call-start = ((), (), s32[]{:S(2)}) async-start(), calls=%async_computation.5 | async-start | bytes 16515072 | tf_op jit(solution)/shard_map/all_gather | solution.py:64
  8.0 144.7 %reduce-scatter.3.cloned.1.call-start = ((), (), s32[]{:S(2)}) async-start(), calls=%async_computation.6 | async-start | bytes 573440 | tf_op jit(solution)/shard_map/reduce_scatter | solution.py:90
  14.7 2.1 copy-start.9
  14.7 25.2 %copy-start.8 = (bf16[1024,576]{0,1:T(8,128)(2,1)S(1)}, bf16[1024,576]{0,1:T(8,128)(2,1)}, u32[]{:S(2)}) copy-start(bf16[1024,576]{0,1:T(8,128)(2,1)} %param.13) | copy-start | bytes 3538948
  46.3 85.5 %copy-start.5 = (s32[64,8]{0,1:T(8,128)S(1)}, s32[64,8]{0,1:T(8,128)}, u32[]{:S(2)}) copy-start(s32[64,8]{0,1:T(8,128)} %param.19) | copy-start | bytes 6148
  46.3 106.4 %copy-start.3 = (bf16[16,3584]{1,0:T(8,128)(2,1)S(1)}, bf16[16,3584]{1,0:T(8,128)(2,1)}, u32[]{:S(2)}) copy-start(bf16[16,3584]{1,0:T(8,128)(2,1)} %param.15) | copy-start | bytes 344068
  46.3 107.4 %copy-start.6 = (f32[3584]{0:T(1024)S(1)}, f32[3584]{0:T(1024)}, u32[]{:S(2)}) copy-start(f32[3584]{0:T(1024)} %param.18) | copy-start | bytes 43012
  277.5 3.0 copy-start.2
  306.9 5.6 %copy-start.7 = (f32[64,8]{0,1:T(8,128)S(1)}, f32[64,8]{0,1:T(8,128)}, u32[]{:S(2)}) copy-start(f32[64,8]{0,1:T(8,128)} %param.20) | copy-start | bytes 6148
  306.9 87.8 %all-to-all-start.1 = ((bf16[8,4,32,3584]{3,2,1,0:T(8,128)(2,1)}), bf16[8,4,32,3584]{3,2,1,0:T(8,128)(2,1)}, u32[]{:S(2)}, u32[]{:S(2)}) async-start(bf16[8,4,32,3584]{3,2,1,0:T(8,128)(2,1)} %copy.51), calls=%async_computation.2 | async-start | bytes 14680064 | tf_op jit(solution)/shard_map/all_to_all | solution.py:40
  311.9 119.4 %reduce-scatter.5.cloned.1.call-start = ((), (), s32[]{:S(2)}) async-start(), calls=%async_computation.7 | async-start | bytes 573440 | tf_op jit(solution)/shard_map/reduce_scatter | solution.py:122
  394.7 36.6 %copy-start.4 = (bf16[16,3584]{1,0:T(8,128)(2,1)S(1)}, bf16[16,3584]{1,0:T(8,128)(2,1)}, u32[]{:S(2)}) copy-start(bf16[16,3584]{1,0:T(8,128)(2,1)} %reduce-scatter.3.cloned.1.call-done) | copy-start | bytes 344068
  394.7 38.1 %copy-start.1 = (bf16[64,16,576]{2,1,0:T(8,128)(2,1)S(1)}, bf16[64,16,576]{2,1,0:T(8,128)(2,1)}, u32[]{:S(2)}) copy-start(bf16[64,16,576]{2,1,0:T(8,128)(2,1)} %param.12) | copy-start | bytes 3538948
Sparse Core Ops, SparseCore 0:
  9.2 30.5 all-gather.2
  41.8 80.9 all-gather.4
  131.5 21.0 reduce-scatter.2
  413.7 17.5 reduce-scatter.4
where the time goes:
time: 447 us; the launch traced here: 440 us
  waiting for transfers between devices  220 us (49%)
  blocking collectives  102 us (23%)
  matrix products  37.9 us (8%)
  other arithmetic  34.1 us (8%)
  local copies, waits for them, and re-layouts  26.8 us (6%)
  between operations  13.7 us (3%)
  starting transfers between devices  5.35 us (1%)
    all_to_all x1, blocking collectives, per_device(): lax.all_to_all(outgoing, 'expert', split_axis=0, concat_axis=0, tiled=True)  86.5 us
    all_to_all x1, waiting for transfers between devices, send_back(): lax.all_to_all(outputs, 'expert', split_axis=0, concat_axis=0, tiled=True)  82.2 us
    all_gather x1, waiting for transfers between devices, per_device(): lax.all_gather(w_out, 'expert', axis=0, tiled=True)  76.5 us
    all_gather x1, waiting for transfers between devices, per_device(): lax.all_gather(w_uv, 'expert', axis=0, tiled=True)  21.6 us
    scatter x1, other arithmetic, per_device(): outgoing = jnp.zeros((experts_all * capacity, model_width), jnp.bfloat16)...  20.8 us
    reduce_scatter x1, waiting for transfers between devices, per_device(): lax.psum_scatter(partial_value.astype(jnp.bfloat16), 'tensor', scatter_di...  20.6 us
    reduce_scatter x1, waiting for transfers between devices, per_device(): lax.psum_scatter(mixed_sum.astype(jnp.bfloat16), 'tensor', scatter_dimens...  17.7 us
    all_gather x1, blocking collectives, per_device(): lax.all_gather(rms_rows(own_hidden, norm_gain), 'tensor', axis=0, tiled=T...  15.5 us
  transfers between devices with their start and end apart: 5, of which 5 were waited for; matrix products, arithmetic and copies ran while one was open for 4% of the time, Pallas kernels for 0%

commit v1 on v0

v1 whole, which is shorter than its diff:
```python
import jax
import jax.numpy as jnp
from jax import lax
from jax.sharding import PartitionSpec as P

LATENT = 512
ROPE = 64
VDIM = 128


EPSILON = 1e-06


def rms_rows(rows, norm_gain):
    scale_rows = lax.rsqrt(jnp.mean(rows * rows, axis=1, keepdims=True) + EPSILON)
    return (rows * scale_rows * norm_gain).astype(jnp.bfloat16)


def attend(queries, latent_cache, new_latents):
    tok_rows = queries.shape[0]
    context = latent_cache.shape[0]
    key_rows = jnp.concatenate([latent_cache, new_latents], axis=0)
    scores = jnp.einsum("thc,kc->htk", queries, key_rows, preferred_element_type=jnp.float32) * (
        VDIM + ROPE
    ) ** (-0.5)
    query_pos = jnp.arange(tok_rows, dtype=jnp.int32)[:, None]
    key_pos = jnp.arange(key_rows.shape[0], dtype=jnp.int32)[None, :] - context
    scores = jnp.where((key_pos <= query_pos)[None], scores, -jnp.inf)
    row_peak = jnp.max(scores, axis=2, keepdims=True)
    exp_scores = jnp.exp(scores - row_peak)
    attn_probs = (exp_scores / jnp.sum(exp_scores, axis=2, keepdims=True)).astype(jnp.bfloat16)
    return jnp.einsum(
        "htk,kl->htl", attn_probs, key_rows[:, :LATENT], preferred_element_type=jnp.float32
    ).astype(jnp.bfloat16)


def per_device(
    queries,
    latent_cache,
    new_latents,
    residual,
    w_uv,
    w_out,
    norm_gain,
    expert_ids,
    gate_weights,
    w_gate,
    w_up,
    w_down,
):
    group_count = lax.axis_size("expert")
    tok_rows = queries.shape[0]
    head_count = queries.shape[1]
    local_experts = w_gate.shape[0]
    experts_all = local_experts * group_count
    everyone = ("expert", "tensor")

    chosen = expert_ids[:, :, None] == jnp.arange(experts_all, dtype=jnp.int32)
    mix = jnp.sum(jnp.where(chosen, gate_weights[:, :, None], 0.0), axis=1)
    mix = lax.all_to_all(
        mix.reshape(tok_rows, group_count, local_experts),
        "expert",
        split_axis=1,
        concat_axis=0,
        tiled=True,
    ).reshape(-1, local_experts)

    uv_rows = lax.all_gather(w_uv, "expert", axis=0, tiled=True)
    attended = attend(queries, latent_cache, new_latents)
    head_values = jnp.einsum(
        "htl,hlv->thv",
        attended,
        uv_rows.reshape(head_count, LATENT, VDIM),
        preferred_element_type=jnp.float32,
    ).astype(jnp.bfloat16)
    columns = head_values.reshape(tok_rows, group_count, -1)
    columns = lax.all_to_all(columns, "expert", split_axis=1, concat_axis=0, tiled=True)
    columns = columns.reshape(group_count * tok_rows, -1)
    share = jnp.dot(columns, w_out, preferred_element_type=jnp.float32).astype(jnp.bfloat16)
    own_hidden = lax.psum_scatter(share, everyone, scatter_dimension=0, tiled=True).astype(
        jnp.float32
    ) + residual.astype(jnp.float32)
    normed = lax.all_gather(rms_rows(own_hidden, norm_gain), everyone, axis=0, tiled=True)

    gate_part = jnp.einsum("nd,edf->enf", normed, w_gate, preferred_element_type=jnp.float32)
    up_part = jnp.einsum("nd,edf->enf", normed, w_up, preferred_element_type=jnp.float32)
    active = (jax.nn.silu(gate_part) * up_part * mix.T[:, :, None]).astype(jnp.bfloat16)
    produced = jnp.einsum("enf,efd->nd", active, w_down, preferred_element_type=jnp.float32)
    summed = lax.psum_scatter(
        produced.astype(jnp.bfloat16), everyone, scatter_dimension=0, tiled=True
    ).astype(jnp.float32)
    return (own_hidden + summed).astype(jnp.bfloat16)


def solution(mesh):
    placed = (
        P("expert", "tensor", None),
        P("expert", None),
        P("expert", None),
        P(("expert", "tensor"), None),
        P(("tensor", "expert"), None),
        P(("tensor", "expert"), None),
        P(),
        P("expert", None),
        P("expert", None),
        P("expert", None, "tensor"),
        P("expert", None, "tensor"),
        P("expert", "tensor", None),
    )
    return jax.shard_map(
        per_device,
        mesh=mesh,
        in_specs=placed,
        out_specs=P(("expert", "tensor"), None),
        check_vma=False,
    )
```

time: 447 us -> 443 us (level); the launches traced: 440 us -> 443 us
  waiting for transfers between devices: 220 us -> 364 us
  blocking collectives: 102 us -> 16.7 us
  other arithmetic: 34.1 us -> 6.38 us
  local copies, waits for them, and re-layouts: 26.8 us -> 4.19 us
  starting transfers between devices: 5.35 us -> 0.12 us
    reduce_scatter x2, waiting for transfers between devices: 38.2 us -> 287 us  [the longest x1 144 us: per_device(): lax.psum_scatter(produced.astype(jnp.bfloat16), everyone, scatter_dimensi...]
    all_to_all x1 -> x0, waiting for transfers between devices: 82.2 us -> none  [send_back(): lax.all_to_all(outputs, 'expert', split_axis=0, concat_axis=0, tiled=True)]
    all_to_all x1 -> x2, blocking collectives: 86.5 us -> 16.7 us  [the longest x1 9.48 us: per_device(): lax.all_to_all(columns, 'expert', split_axis=1, concat_axis=0, tiled=True)]
    all_gather x2, waiting for transfers between devices: 98.1 us -> 75.3 us  [the longest x1 51.2 us: per_device(): lax.all_gather(rms_rows(own_hidden, norm_gain), everyone, axis=0, tiled=T...]
    scatter x1 -> x0, other arithmetic: 20.8 us -> none  [per_device(): outgoing = jnp.zeros((experts_all * capacity, model_width), jnp.bfloat16)...]
    all_gather x1 -> x0, blocking collectives: 15.5 us -> none  [per_device(): lax.all_gather(rms_rows(own_hidden, norm_gain), 'tensor', axis=0, tiled=T...]
    gather x1 -> x0, local copies, waits for them, and re-layouts: 12 us -> none  [per_device(): jnp.take(result.reshape(experts_all * capacity, model_width), slot_index,...]
    reduce_sum x2 -> x1, other arithmetic: 6.9 us -> 0.03 us  [per_device(): mix = jnp.sum(jnp.where(chosen, gate_weights[:, :, None], 0.0), axis=1)]
  transfers between devices with their start and end apart: 5 -> 4, of which waited for: 5 -> 4; matrix products, arithmetic and copies ran while one was open for 4% -> 2% of each run, Pallas kernels for 0% -> 0%
where the time goes in v1:
time: 443 us
  waiting for transfers between devices  364 us (82%)
  matrix products  38.3 us (9%)
  blocking collectives  16.7 us (4%)
  between operations  13.2 us (3%)
  other arithmetic  6.38 us (1%)
    reduce_scatter x1, waiting for transfers between devices, per_device(): lax.psum_scatter(produced.astype(jnp.bfloat16), everyone, scatter_dimensi...  144 us
    reduce_scatter x1, waiting for transfers between devices, per_device(): lax.psum_scatter(share, everyone, scatter_dimension=0, tiled=True)  144 us
    all_gather x1, waiting for transfers between devices, per_device(): lax.all_gather(rms_rows(own_hidden, norm_gain), everyone, axis=0, tiled=T...  51.2 us
    all_gather x1, waiting for transfers between devices, per_device(): uv_rows = lax.all_gather(w_uv, 'expert', axis=0, tiled=True)  24.1 us
    dot_general x1, matrix products, per_device(): jnp.einsum('enf,efd->nd', active, w_down, preferred_element_type=jnp.floa...  16.5 us
    dot_general x1, matrix products, per_device(): jnp.einsum('nd,edf->enf', normed, w_gate, preferred_element_type=jnp.floa...  9.53 us
    all_to_all x1, blocking collectives, per_device(): lax.all_to_all(columns, 'expert', split_axis=1, concat_axis=0, tiled=True)  9.48 us
  transfers between devices with their start and end apart: 4, of which 4 were waited for; matrix products, arithmetic and copies ran while one was open for 2% of the time, Pallas kernels for 0%

profile of v1, /device:TPU:0, one launch (start us, length us, event | category | flops | bytes accessed | tf_op | source)
XLA Modules:
  0.0 442.5 jit_solution(3831684272246391580)
XLA Ops:
  6.5 0.0 copy-start
  6.5 0.0 all-gather.3.cloned.1.call-start
  6.5 0.7 all-gather.3.cloned.1.call-update
  7.3 0.0 reduce-scatter.3.cloned.1.call-start
  7.3 1.0 copy.39
  8.3 3.9 convolution_multiply_fusion
  12.2 0.0 copy-start.6
  12.3 2.1 copy-done.6
  14.4 1.5 exponential_reduce_fusion
  15.8 24.1 %all-gather.3.cloned.1.call-done = bf16[8192,128]{1,0:T(8,128)(2,1)} async-done(((bf16[1024,128]{1,0:T(8,128)(2,1)}), bf16[8192,128]{1,0:T(8,128)(2,1)}) %all-gather.3.cloned.1.call-update) | async-done | bytes 2097168 | tf_op jit(solution)/shard_map/all_gather | solution.py:68
  39.9 5.5 %fusion.30 = bf16[64,16,128]{2,0,1:T(8,128)(2,1)S(1)} fusion(bf16[16,512,128]{2,1,0:T(8,128)(2,1)} %bitcast.86, f32[16,64]{1,0:T(8,128)S(1)} %exponential_reduce_fusion, bf16[1024,576]{0,1:T(8,128)(2,1)} %param.13, bf16[64,576]{0,1:T(8,128)(2,1)S(1)} %copy.39, f32[1088,64,16]{0,1,2:T(8,128)} %copy-done.6, pred[64,1088]{1,0:T(8,128)(4,1)S(1)} %iota_compare_fusion), kind=kOutput, calls=%fused_computation.35 | convolution fusion | flops 1282410496 | bytes 8142848 | tf_op jit(solution)/shard_map/htl,hlv->thv/dot_general | solution.py:70
  45.4 0.2 copy.42
  45.6 0.1 reshape.57
  45.7 9.5 %all_to_all.30 = bf16[64,8,256]{2,0,1:T(8,128)(2,1)S(1)} all-to-all(bf16[64,8,256]{2,0,1:T(8,128)(2,1)S(1)} %copy.43), channel_id=1, replica_groups=mesh['tensor'=4,'expert'=8] {'expert'}, dimensions={1} | all-to-all | bytes 524288 | tf_op jit(solution)/shard_map/all_to_all | solution.py:77
  55.2 0.0 copy-done
  55.2 2.9 convolution_convert_fusion
  58.1 0.0 copy-start.1
  58.1 0.0 copy-start.3
  58.1 0.0 copy-start.4
  58.1 0.0 copy-start.5
  58.1 0.0 reduce-scatter.3.cloned.1.call-update
  58.2 0.0 all-gather.5.cloned.1.call-start
  58.2 143.6 %reduce-scatter.3.cloned.1.call-done = bf16[16,3584]{1,0:T(8,128)(2,1)} async-done(((bf16[512,3584]{1,0:T(8,128)(2,1)}), bf16[16,3584]{1,0:T(8,128)(2,1)}) %reduce-scatter.3.cloned.1.call-update) | async-done | bytes 114704 | tf_op jit(solution)/shard_map/reduce_scatter | solution.py:80
  201.9 0.0 copy-done.1
  201.9 1.0 multiply_reduce_fusion
  202.9 0.0 copy-done.3
  202.9 1.6 multiply_convert_fusion
  204.6 0.0 all-gather.5.cloned.1.call-update
  204.6 0.0 reduce-scatter.5.cloned.1.call-start
  204.6 0.0 copy-done.4
  204.6 0.0 copy-done.5
  204.7 0.1 reshape.65
  204.8 7.3 %all_to_all.31 = f32[8,1,256]{2,1,0:T(1,128)S(1)} all-to-all(f32[8,1,256]{2,1,0:T(1,128)S(1)} %reshape.65), channel_id=1, replica_groups=mesh['tensor'=4,'expert'=8] {'expert'}, dimensions={0} | all-to-all | bytes 16384 | tf_op jit(solution)/shard_map/all_to_all | solution.py:60
  212.0 0.5 broadcast.54
  212.5 0.6 reduce
  213.1 0.1 reshape.66
  213.2 0.1 reshape.60
  213.3 51.2 %all-gather.5.cloned.1.call-done = bf16[512,3584]{1,0:T(8,128)(2,1)} async-done(((bf16[16,3584]{1,0:T(8,128)(2,1)}), bf16[512,3584]{1,0:T(8,128)(2,1)}) %all-gather.5.cloned.1.call-update) | async-done | bytes 3670032 | tf_op jit(solution)/shard_map/all_gather | solution.py:83
  264.5 9.5 %fusion.5 = f32[512,4,256]{2,0,1:T(8,128)} fusion(bf16[4,3584,256]{2,1,0:T(8,128)(2,1)} %param.21, bf16[512,3584]{1,0:T(8,128)(2,1)} %all-gather.5.cloned.1.call-done), kind=kOutput, calls=%fused_computation.11 | convolution fusion | flops 3758096384 | bytes 13107200 | tf_op jit(solution)/shard_map/nd,edf->enf/dot_general | solution.py:85
  274.1 16.5 %bitcast_convert_fusion = bf16[512,3584]{1,0:T(8,128)(2,1)} fusion(bf16[4,256,3584]{2,1,0:T(8,128)(2,1)} %param.23, f32[512,4,256]{2,0,1:T(8,128)} %fusion.5, bf16[4,3584,256]{2,1,0:T(8,128)(2,1)} %param.22, bf16[512,3584]{1,0:T(8,128)(2,1)} %all-gather.5.cloned.1.call-done, f32[4,512]{1,0:T(4,128)S(1)} %bitcast.85), kind=kOutput, calls=%fused_computation.1 | convolution fusion | flops 7521697792 | bytes 24125440 | tf_op jit(solution)/shard_map/enf,efd->nd/dot_general | solution.py:88
  290.5 0.0 copy-start.2
  290.5 0.0 reduce-scatter.5.cloned.1.call-update
  290.6 143.8 %reduce-scatter.5.cloned.1.call-done = bf16[16,3584]{1,0:T(8,128)(2,1)} async-done(((bf16[512,3584]{1,0:T(8,128)(2,1)}), bf16[16,3584]{1,0:T(8,128)(2,1)}) %reduce-scatter.5.cloned.1.call-update) | async-done | bytes 114704 | tf_op jit(solution)/shard_map/reduce_scatter | solution.py:89
  434.4 0.0 copy-done.2
  434.4 1.6 add_convert_fusion
  (7 shorter events, 0.1 us)
Async XLA Ops:
  6.5 48.7 %copy-start = (bf16[256,3584]{1,0:T(8,128)(2,1)S(1)}, bf16[256,3584]{1,0:T(8,128)(2,1)}, u32[]{:S(2)}) copy-start(bf16[256,3584]{1,0:T(8,128)(2,1)} %param.17) | copy-start | bytes 5505028
  6.5 33.3 %all-gather.3.cloned.1.call-start = ((), (), s32[]{:S(2)}) async-start(), calls=%async_computation.4 | async-start | bytes 2359296 | tf_op jit(solution)/shard_map/all_gather | solution.py:68
  7.3 194.6 %reduce-scatter.3.cloned.1.call-start = ((), (), s32[]{:S(2)}) async-start(), calls=%async_computation.5 | async-start | bytes 3784704 | tf_op jit(solution)/shard_map/reduce_scatter | solution.py:80
  12.2 2.1 copy-start.6
  58.1 143.7 %copy-start.1 = (bf16[16,3584]{1,0:T(8,128)(2,1)S(1)}, bf16[16,3584]{1,0:T(8,128)(2,1)}, u32[]{:S(2)}) copy-start(bf16[16,3584]{1,0:T(8,128)(2,1)} %param.15) | copy-start | bytes 344068
  58.1 144.8 %copy-start.3 = (f32[3584]{0:T(1024)S(1)}, f32[3584]{0:T(1024)}, u32[]{:S(2)}) copy-start(f32[3584]{0:T(1024)} %param.18) | copy-start | bytes 43012
  58.1 146.5 %copy-start.4 = (f32[64,8]{0,1:T(8,128)S(1)}, f32[64,8]{0,1:T(8,128)}, u32[]{:S(2)}) copy-start(f32[64,8]{0,1:T(8,128)} %param.20) | copy-start | bytes 6148
  58.1 146.5 %copy-start.5 = (s32[64,8]{0,1:T(8,128)S(1)}, s32[64,8]{0,1:T(8,128)}, u32[]{:S(2)}) copy-start(s32[64,8]{0,1:T(8,128)} %param.19) | copy-start | bytes 6148
  58.2 206.4 %all-gather.5.cloned.1.call-start = ((), (), s32[]{:S(2)}) async-start(), calls=%async_computation.6 | async-start | bytes 3784704 | tf_op jit(solution)/shard_map/all_gather | solution.py:83
  204.6 229.8 %reduce-scatter.5.cloned.1.call-start = ((), (), s32[]{:S(2)}) async-start(), calls=%async_computation.7 | async-start | bytes 3784704 | tf_op jit(solution)/shard_map/reduce_scatter | solution.py:89
  290.5 143.9 %copy-start.2 = (bf16[16,3584]{1,0:T(8,128)(2,1)S(1)}, bf16[16,3584]{1,0:T(8,128)(2,1)}, u32[]{:S(2)}) copy-start(bf16[16,3584]{1,0:T(8,128)(2,1)} %reduce-scatter.3.cloned.1.call-done) | copy-start | bytes 344068
Sparse Core Ops, SparseCore 0:
  9.2 30.5 all-gather.2
  58.3 143.5 reduce-scatter.2
  205.1 59.3 all-gather.4
  290.7 143.6 reduce-scatter.4

commit v2 on v1

--- a/solution.py
+++ b/solution.py
@@ -1,6 +1,10 @@
+import functools
+
 import jax
 import jax.numpy as jnp
 from jax import lax
+from jax.experimental import pallas as pl
+from jax.experimental.pallas import tpu as pltpu
 from jax.sharding import PartitionSpec as P
 
 LATENT = 512
@@ -11,9 +15,210 @@
 EPSILON = 1e-06
 
 
-def rms_rows(rows, norm_gain):
-    scale_rows = lax.rsqrt(jnp.mean(rows * rows, axis=1, keepdims=True) + EPSILON)
-    return (rows * scale_rows * norm_gain).astype(jnp.bfloat16)
+MESH = pl.DeviceIdType.MESH
+VMEM_BYTES = 60 * 2**20
+
+
+def stage_orders(experts_n, tensor_n):
+    e_bits = [("expert", 1 << k) for k in range(experts_n.bit_length() - 1)]
+    t_bits = [("tensor", 1 << k) for k in range(tensor_n.bit_length() - 1)]
+    core, plane = e_bits[:1], e_bits[1:]
+    return (
+        core + plane + t_bits,
+        core + plane[1:] + t_bits + plane[:1],
+        core + t_bits + plane,
+    )
+
+
+def piece_columns(width, count):
+    units = width // 256
+    sizes = [(units + count - 1 - i) // count * 256 for i in range(count)]
+    sizes[0] += width - sum(sizes)
+    return [(sum(sizes[:i]), sizes[i]) for i in range(count)]
+
+
+def natural_dim(stage, experts_n, tensor_n):
+    axis, stride = stage
+    e_bits, t_bits = experts_n.bit_length() - 1, tensor_n.bit_length() - 1
+    last = e_bits if axis == "expert" else e_bits + t_bits
+    return last - stride.bit_length()
+
+
+def in_order(rows, order, experts_n, tensor_n):
+    bits = len(order)
+    block = rows.shape[0] >> bits
+    split = rows.reshape((2,) * bits + (block, rows.shape[1]))
+    dims = [natural_dim(s, experts_n, tensor_n) for s in order]
+    return split.transpose(dims + [bits, bits + 1]).reshape(rows.shape)
+
+
+def my_bit(stage):
+    return lax.rem(lax.axis_index(stage[0]) // stage[1], 2)
+
+
+def partner(stage):
+    axis, stride = stage
+    return {axis: lax.axis_index(axis) + stride * (1 - 2 * my_bit(stage))}
+
+
+def greet(stages):
+    barrier = pltpu.get_barrier_semaphore()
+    for stage in stages:
+        pl.semaphore_signal(barrier, inc=1, device_id=partner(stage), device_id_type=MESH)
+    pl.semaphore_wait(barrier, len(stages))
+
+
+def project(lhs_ref, w_ref, buf, start):
+    blocks, block, width = buf.shape
+
+    @pl.loop(0, width // 256)
+    def _(c):
+        off = pl.multiple_of(c * 256, 256)
+        tile = jnp.dot(
+            lhs_ref[...],
+            w_ref[:, pl.ds(pl.multiple_of(start + off, 256), 256)],
+            preferred_element_type=jnp.float32,
+        )
+        buf[:, :, pl.ds(off, 256)] = tile.reshape(blocks, block, 256).astype(buf.dtype)
+
+
+def halve(order, step, low, buf, got, send_sem, recv_sem):
+    half = buf.shape[0] >> (step + 1)
+    bit = my_bit(order[step])
+    at = buf.shape[0] - 2 * half
+    copy = pltpu.make_async_remote_copy(
+        src_ref=buf.at[pl.ds(low + (1 - bit) * half, half)],
+        dst_ref=got.at[pl.ds(at, half)],
+        send_sem=send_sem.at[step],
+        recv_sem=recv_sem.at[step],
+        device_id=partner(order[step]),
+        device_id_type=MESH,
+    )
+    copy.start()
+    return copy, low + bit * half
+
+
+def reduce_scatter(orders, columns, lhs, w_ref, bufs, gots, send_sem, recv_sem, finish):
+    count = len(orders)
+    held, pending = [], []
+    for p in range(count):
+        project(lhs[p], w_ref, bufs[p], columns[p][0])
+        copy, low = halve(orders[p], 0, 0, bufs[p], gots[p], send_sem.at[p], recv_sem.at[p])
+        pending.append(copy)
+        held.append(low)
+    steps = len(orders[0])
+    started = list(pending)
+    for step in range(steps):
+        for p in range(count):
+            pending[p].wait_recv()
+            half = bufs[p].shape[0] >> (step + 1)
+            at = bufs[p].shape[0] - 2 * half
+            if step == steps - 1:
+                total = bufs[p][held[p]].astype(jnp.float32) + gots[p][at].astype(jnp.float32)
+                finish(p, total)
+                continue
+
+            def add(i, _, p=p, at=at, low=held[p]):
+                mine = bufs[p][low + i].astype(jnp.float32)
+                bufs[p][low + i] = (mine + gots[p][at + i].astype(jnp.float32)).astype(jnp.bfloat16)
+                return 0
+
+            lax.fori_loop(0, half, add, 0)
+            pending[p], held[p] = halve(
+                orders[p], step + 1, held[p], bufs[p], gots[p], send_sem.at[p], recv_sem.at[p]
+            )
+            started.append(pending[p])
+    for copy in started:
+        copy.wait_send()
+
+
+def attention_out_kernel(
+    orders, columns, sizes, l0, l1, l2, w_ref, res_ref, gain_ref, hid_ref, all_ref,
+    b0, b1, b2, g0, g1, g2, a0, a1, a2, send_sem, recv_sem, ag_send, ag_recv,
+):
+    greet(orders[0])
+    bits = len(orders[0])
+
+    def finish(p, total):
+        cols = pl.ds(*columns[p])
+        hid_ref[:, cols] = total + res_ref[:, cols].astype(jnp.float32)
+
+    reduce_scatter(
+        orders, columns, (l0, l1, l2), w_ref, (b0, b1, b2), (g0, g1, g2), send_sem, recv_sem, finish
+    )
+    rows = hid_ref[...]
+    scale = lax.rsqrt(jnp.mean(rows * rows, axis=1, keepdims=True) + EPSILON)
+    held, copies = [], []
+    gathered = (a0, a1, a2)
+    for p, order in enumerate(orders):
+        place = 0
+        for stage in order:
+            place = place * 2 + my_bit(stage)
+        cols = pl.ds(*columns[p])
+        gathered[p][place] = (hid_ref[:, cols] * scale * gain_ref[:, cols]).astype(jnp.bfloat16)
+        held.append(place)
+    for step in range(bits):
+        for p, order in enumerate(orders):
+            stage = order[bits - 1 - step]
+            if step:
+                copies[-len(orders)].wait_recv()
+            part = gathered[p].at[pl.ds(held[p], 1 << step)]
+            copy = pltpu.make_async_remote_copy(
+                src_ref=part,
+                dst_ref=part,
+                send_sem=ag_send.at[p, step],
+                recv_sem=ag_recv.at[p, step],
+                device_id=partner(stage),
+                device_id_type=MESH,
+            )
+            copy.start()
+            copies.append(copy)
+            held[p] = held[p] - my_bit(stage) * (1 << step)
+    for p, order in enumerate(orders):
+        copies[p - len(orders)].wait_recv()
+
+        def place_block(i, _, p=p, order=order):
+            natural = 0
+            for k, stage in enumerate(order):
+                dim = natural_dim(stage, *sizes)
+                natural = natural + lax.rem(i // (1 << (bits - 1 - k)), 2) * (1 << (bits - 1 - dim))
+            all_ref[natural, :, pl.ds(*columns[p])] = gathered[p][i]
+            return 0
+
+        lax.fori_loop(0, 1 << bits, place_block, 0)
+    for copy in copies:
+        copy.wait_send()
+
+
+def down_kernel(
+    orders, columns, l0, l1, l2, w_ref, hid_ref, out_ref, b0, b1, b2, g0, g1, g2, send_sem, recv_sem
+):
+    greet(orders[0])
+
+    def finish(p, total):
+        cols = pl.ds(*columns[p])
+        out_ref[:, cols] = (hid_ref[:, cols] + total).astype(out_ref.dtype)
+
+    reduce_scatter(
+        orders, columns, (l0, l1, l2), w_ref, (b0, b1, b2), (g0, g1, g2), send_sem, recv_sem, finish
+    )
+
+
+def call(kernel, collective_id, args, outs, blocks, block, columns, gathers, steps, cost):
+    vmem = pl.BlockSpec(memory_space=pltpu.VMEM)
+    bufs = [pltpu.VMEM((blocks, block, w), jnp.bfloat16) for _, w in columns]
+    sems = [pltpu.SemaphoreType.DMA((len(columns), steps))] * (4 if gathers else 2)
+    return pl.pallas_call(
+        kernel,
+        out_shape=outs,
+        in_specs=[vmem] * len(args),
+        out_specs=jax.tree.map(lambda _: vmem, outs),
+        scratch_shapes=bufs * (3 if gathers else 2) + sems,
+        compiler_params=pltpu.CompilerParams(
+            collective_id=collective_id, has_side_effects=True, vmem_limit_bytes=VMEM_BYTES
+        ),
+        cost_estimate=cost,
+    )(*args)
 
 
 def attend(queries, latent_cache, new_latents):
@@ -76,20 +281,49 @@
     columns = head_values.reshape(tok_rows, group_count, -1)
     columns = lax.all_to_all(columns, "expert", split_axis=1, concat_axis=0, tiled=True)
     columns = columns.reshape(group_count * tok_rows, -1)
-    share = jnp.dot(columns, w_out, preferred_element_type=jnp.float32).astype(jnp.bfloat16)
-    own_hidden = lax.psum_scatter(share, everyone, scatter_dimension=0, tiled=True).astype(
-        jnp.float32
-    ) + residual.astype(jnp.float32)
-    normed = lax.all_gather(rms_rows(own_hidden, norm_gain), everyone, axis=0, tiled=True)
-
-    gate_part = jnp.einsum("nd,edf->enf", normed, w_gate, preferred_element_type=jnp.float32)
-    up_part = jnp.einsum("nd,edf->enf", normed, w_up, preferred_element_type=jnp.float32)
-    active = (jax.nn.silu(gate_part) * up_part * mix.T[:, :, None]).astype(jnp.bfloat16)
-    produced = jnp.einsum("enf,efd->nd", active, w_down, preferred_element_type=jnp.float32)
-    summed = lax.psum_scatter(
-        produced.astype(jnp.bfloat16), everyone, scatter_dimension=0, tiled=True
-    ).astype(jnp.float32)
-    return (own_hidden + summed).astype(jnp.bfloat16)
+    tensor_n = lax.axis_size("tensor")
+    sizes = (group_count, tensor_n)
+    orders = stage_orders(*sizes)
+    model_width = residual.shape[1]
+    cut = piece_columns(model_width, len(orders))
+    blocks = group_count * tensor_n
+    block = residual.shape[0]
+    steps = len(orders[0])
+    flops = 2 * blocks * block * w_out.size
+    own_hidden, normed = call(
+        functools.partial(attention_out_kernel, orders, cut, sizes),
+        0,
+        [in_order(columns, o, *sizes) for o in orders]
+        + [w_out, residual, norm_gain.reshape(1, model_width)],
+        (
+            jax.ShapeDtypeStruct((block, model_width), jnp.float32),
+            jax.ShapeDtypeStruct((blocks, block, model_width), jnp.bfloat16),
+        ),
+        blocks,
+        block,
+        cut,
+        True,
+        steps,
+        pl.CostEstimate(flops=flops, bytes_accessed=w_out.size * 2, transcendentals=0),
+    )
+    normed = normed.reshape(blocks * block, model_width)
+
+    gate_part = jnp.einsum("nd,edf->nef", normed, w_gate, preferred_element_type=jnp.float32)
+    up_part = jnp.einsum("nd,edf->nef", normed, w_up, preferred_element_type=jnp.float32)
+    active = (jax.nn.silu(gate_part) * up_part * mix[:, :, None]).astype(jnp.bfloat16)
+    active = active.reshape(blocks * block, -1)
+    return call(
+        functools.partial(down_kernel, orders, cut),
+        1,
+        [in_order(active, o, *sizes) for o in orders] + [w_down.reshape(-1, model_width), own_hidden],
+        jax.ShapeDtypeStruct((block, model_width), jnp.bfloat16),
+        blocks,
+        block,
+        cut,
+        False,
+        steps,
+        pl.CostEstimate(flops=2 * blocks * block * w_down.size, bytes_accessed=w_down.size * 2, transcendentals=0),
+    )
 
 
 def solution(mesh):

time: 443 us -> 190 us (0.43)
  waiting for transfers between devices: 364 us -> 23.3 us
  Pallas kernels: 0 us -> 102 us
  blocking collectives: 16.7 us -> 0 us
  matrix products: 38.3 us -> 23.6 us
  local copies, waits for them, and re-layouts: 4.19 us -> 14.7 us
  starting transfers between devices: 0.12 us -> 8.76 us
    reduce_scatter x2 -> x0, waiting for transfers between devices: 287 us -> none  [the longest x1 144 us: per_device(): lax.psum_scatter(produced.astype(jnp.bfloat16), everyone, scatter_dimensi...]
    pallas_call x0 -> x2, Pallas kernels: none -> 102 us  [call(): pl.pallas_call(kernel, out_shape=outs, in_specs=[vmem] * len(args), out_s...]
    all_gather x1 -> x0, waiting for transfers between devices: 51.2 us -> none  [per_device(): lax.all_gather(rms_rows(own_hidden, norm_gain), everyone, axis=0, tiled=T...]
    all_to_all x2 -> x0, blocking collectives: 16.7 us -> none  [the longest x1 9.48 us: per_device(): lax.all_to_all(columns, 'expert', split_axis=1, concat_axis=0, tiled=True)]
    dot_general x3 -> x2, matrix products: 28.9 us -> 14.8 us  [the longest x1 7.45 us: per_device(): jnp.einsum('nd,edf->nef', normed, w_up, preferred_element_type=jnp.float32)]
    all_to_all x0 -> x2, starting transfers between devices: none -> 8.76 us  [the longest x1 5.17 us: per_device(): lax.all_to_all(mix.reshape(tok_rows, group_count, local_experts), 'expert...]
    all_gather x1, waiting for transfers between devices: 24.1 us -> 17.9 us  [per_device(): uv_rows = lax.all_gather(w_uv, 'expert', axis=0, tiled=True)]
    transpose x0 -> x6, local copies, waits for them, and re-layouts: none -> 5.42 us  [in_order(): return split.transpose(dims + [bits, bits + 1]).reshape(rows.shape)]
  transfers between devices with their start and end apart: 4 -> 3, of which waited for: 4 -> 2; matrix products, arithmetic and copies ran while one was open for 2% -> 8% of each run, Pallas kernels for 0% -> 0%
where the time goes in v2:
time: 190 us; the launch traced here: 189 us
  Pallas kernels  102 us (54%)
  matrix products  23.6 us (12%)
  waiting for transfers between devices  23.3 us (12%)
  local copies, waits for them, and re-layouts  14.7 us (8%)
  between operations  13.5 us (7%)
  starting transfers between devices  8.76 us (5%)
  other arithmetic  2.88 us (2%)
    pallas_call x2, Pallas kernels, call(): pl.pallas_call(kernel, out_shape=outs, in_specs=[vmem] * len(args), out_s...  102 us
    all_gather x1, waiting for transfers between devices, per_device(): uv_rows = lax.all_gather(w_uv, 'expert', axis=0, tiled=True)  17.9 us
    dot_general x1, matrix products, per_device(): jnp.einsum('nd,edf->nef', normed, w_up, preferred_element_type=jnp.float32)  7.45 us
    dot_general x1, matrix products, per_device(): jnp.einsum('nd,edf->nef', normed, w_gate, preferred_element_type=jnp.floa...  7.32 us
    unnamed x14, local copies, waits for them, and re-layouts  5.42 us
    transpose x6, local copies, waits for them, and re-layouts, in_order(): return split.transpose(dims + [bits, bits + 1]).reshape(rows.shape)  5.42 us
    dot_general x1, matrix products, per_device(): jnp.einsum('htl,hlv->thv', attended, uv_rows.reshape(head_count, LATENT,...  5.29 us
    all_to_all x1, starting transfers between devices, per_device(): lax.all_to_all(mix.reshape(tok_rows, group_count, local_experts), 'expert...  5.17 us
  transfers between devices with their start and end apart: 3, of which 2 were waited for; matrix products, arithmetic and copies ran while one was open for 8% of the time, Pallas kernels for 0%

profile of v2, /device:TPU:0, one launch (start us, length us, event | category | flops | bytes accessed | tf_op | source)
XLA Modules:
  0.0 189.2 jit_solution(8746222998386220)
XLA Ops:
  6.5 0.0 copy-start
  6.5 0.0 all-gather.2.cloned.1.call-start
  6.5 0.7 all-gather.2.cloned.1.call-update
  7.3 0.7 select_reduce_fusion
  8.0 0.7 reshape.83
  8.7 5.2 %all-to-all-start.1 = ((f32[8,1,256]{2,1,0:T(1,128)}), f32[8,1,256]{2,1,0:T(1,128)S(1)}, u32[]{:S(2)}, u32[]{:S(2)}) async-start(f32[8,1,256]{2,1,0:T(1,128)} %reshape.83), calls=%async_computation.1 | async-start | bytes 16384 | tf_op jit(solution)/shard_map/all_to_all | solution.py:265
  13.8 1.0 copy.64
  14.9 0.0 copy-done
  14.9 3.5 %convolution_multiply_fusion = f32[1088,64,16]{0,1,2:T(8,128)S(1)} fusion(bf16[64,576]{0,1:T(8,128)(2,1)S(1)} %copy.64, bf16[64,16,576]{2,1,0:T(8,128)(2,1)S(1)} %copy-done, bf16[1024,576]{0,1:T(8,128)(2,1)} %param.13), kind=kOutput, calls=%fused_computation.2 | convolution fusion | flops 1287077888 | bytes 6889472 | tf_op jit(solution)/shard_map/thc,kc->htk/dot_general | solution.py:228
  18.4 0.0 copy-start.4
  18.5 2.1 %copy-done.4 = f32[1088,64,16]{0,1,2:T(8,128)} copy-done((f32[1088,64,16]{0,1,2:T(8,128)}, f32[1088,64,16]{0,1,2:T(8,128)S(1)}, u32[]{:S(2)}) %copy-start.4) | copy-done | bytes 4456472
  20.5 0.0 copy-start.2
  20.5 1.5 exponential_reduce_fusion
  22.0 17.9 %all-gather.2.cloned.1.call-done = bf16[8192,128]{1,0:T(8,128)(2,1)} async-done(((bf16[1024,128]{1,0:T(8,128)(2,1)}), bf16[8192,128]{1,0:T(8,128)(2,1)}) %all-gather.2.cloned.1.call-update) | async-done | bytes 2097168 | tf_op jit(solution)/shard_map/all_gather | solution.py:273
  39.9 0.0 copy-done.2
  39.9 0.0 copy-start.1
  39.9 5.3 %fusion.17 = bf16[64,16,128]{2,0,1:T(8,128)(2,1)S(1)} fusion(bf16[16,512,128]{2,1,0:T(8,128)(2,1)} %bitcast.80, f32[16,64]{1,0:T(8,128)S(1)} %exponential_reduce_fusion, bf16[1024,576]{0,1:T(8,128)(2,1)S(1)} %copy-done.2, bf16[64,576]{0,1:T(8,128)(2,1)S(1)} %copy.64, f32[1088,64,16]{0,1,2:T(8,128)} %copy-done.4, pred[64,1088]{1,0:T(8,128)(4,1)S(1)} %iota_compare_fusion), kind=kOutput, calls=%fused_computation.22 | convolution fusion | flops 1282410496 | bytes 8142848 | tf_op jit(solution)/shard_map/htl,hlv->thv/dot_general | solution.py:275
  45.2 0.2 copy.67
  45.4 0.1 reshape.69
  45.5 0.7 copy.68
  46.2 0.0 all-to-all-done.1
  46.2 3.6 %all-to-all-start = ((bf16[64,8,256]{2,0,1:T(8,128)(2,1)}), bf16[64,8,256]{2,0,1:T(8,128)(2,1)S(1)}, u32[]{:S(2)}, u32[]{:S(2)}) async-start(bf16[64,8,256]{2,0,1:T(8,128)(2,1)} %copy.68), calls=%async_computation | async-start | bytes 524288 | tf_op jit(solution)/shard_map/all_to_all | solution.py:282
  49.8 0.0 copy-done.1
  49.8 0.6 reshape.73.gain_ref
  50.4 0.6 broadcast.31
  51.0 0.6 reduce
  51.6 0.1 reshape.84
  51.7 0.1 mul.31
  51.8 4.7 %all-to-all-done = bf16[64,8,256]{2,0,1:T(8,128)(2,1)S(1)} async-done(((bf16[64,8,256]{2,0,1:T(8,128)(2,1)}), bf16[64,8,256]{2,0,1:T(8,128)(2,1)S(1)}, u32[]{:S(2)}, u32[]{:S(2)}) %all-to-all-start) | async-done | bytes 262176 | tf_op jit(solution)/shard_map/all_to_all | solution.py:282
  56.5 0.7 copy.70
  57.2 0.7 copy.71
  57.9 0.7 copy.69
  58.7 62.2 %shard_map.118 = (f32[16,3584]{1,0:T(8,128)}, bf16[32,16,3584]{2,1,0:T(8,128)(2,1)}) custom-call(bf16[512,256]{1,0:T(8,128)(2,1)} %bitcast.77, bf16[512,256]{1,0:T(8,128)(2,1)} %bitcast.75, bf16[512,256]{1,0:T(8,128)(2,1)} %bitcast.76, bf16[256,3584]{1,0:T(8,128)(2,1)} %w_ref.1, bf16[16,3584]{1,0:T(8,128)(2,1)} %res_ref.1, f32[1,3584]{1,0:T(1,128)} %reshape.73.gain_ref), custom_call_target="tpu_custom_call" | custom-call | flops 939524096 | bytes 1835008 | tf_op jit(solution)/shard_map/pallas_call | solution.py:211
  120.9 0.0 copy-start.3
  120.9 7.5 %fusion.27 = f32[512,4,256]{2,0,1:T(8,128)S(1)} fusion(bf16[512,3584,1]{1,0,2:T(8,128)(2,1)} %bitcast.81, bf16[4,3584,256]{2,1,0:T(8,128)(2,1)} %param.22), kind=kOutput, calls=%fused_computation.32 | convolution fusion | flops 3758096384 | bytes 13107200 | tf_op jit(solution)/shard_map/nd,edf->nef/dot_general | solution.py:312
  128.4 0.0 copy-done.3
  128.4 7.3 %multiply_convert_fusion = bf16[512,4,256]{2,0,1:T(8,128)(2,1)S(1)} fusion(f32[512,4,256]{2,0,1:T(8,128)S(1)} %fusion.27, bf16[512,3584,1]{1,0,2:T(8,128)(2,1)S(1)} %bitcast.82, bf16[4,3584,256]{2,1,0:T(8,128)(2,1)} %param.21, f32[512,4]{0,1:T(4,128)S(1)} %mul.31), kind=kOutput, calls=%fused_computation.10 | convolution fusion | flops 3761766400 | bytes 14163968 | tf_op jit(solution)/shard_map/nd,edf->nef/dot_general | solution.py:311
  135.7 0.8 copy.73
  136.5 0.8 reshape_reshape.5
  137.3 1.1 copy.74
  138.4 1.1 copy.75
  139.5 1.1 copy.76
  140.5 40.2 %shard_map.119 = bf16[16,3584]{1,0:T(8,128)(2,1)} custom-call(bf16[512,1024]{1,0:T(8,128)(2,1)} %bitcast.72, bf16[512,1024]{1,0:T(8,128)(2,1)} %bitcast.73, bf16[512,1024]{1,0:T(8,128)(2,1)} %bitcast.74, bf16[1024,3584]{1,0:T(8,128)(2,1)} %bitcast.79, f32[16,3584]{1,0:T(8,128)} %get-tuple-element.8.hid_ref), custom_call_target="tpu_custom_call" | custom-call | flops 3758096384 | bytes 7340032 | tf_op jit(solution)/shard_map/pallas_call | solution.py:211
  180.8 1.6 copy.82
  (4 shorter events, 0.1 us)
Async XLA Ops:
  6.5 8.3 %copy-start = (bf16[64,16,576]{2,1,0:T(8,128)(2,1)S(1)}, bf16[64,16,576]{2,1,0:T(8,128)(2,1)}, u32[]{:S(2)}) copy-start(bf16[64,16,576]{2,1,0:T(8,128)(2,1)} %param.12) | copy-start | bytes 3538948
  6.5 33.3 %all-gather.2.cloned.1.call-start = ((), (), s32[]{:S(2)}) async-start(), calls=%async_computation.2 | async-start | bytes 2359296 | tf_op jit(solution)/shard_map/all_gather | solution.py:273
  8.7 37.5 %all-to-all-start.1 = ((f32[8,1,256]{2,1,0:T(1,128)}), f32[8,1,256]{2,1,0:T(1,128)S(1)}, u32[]{:S(2)}, u32[]{:S(2)}) async-start(f32[8,1,256]{2,1,0:T(1,128)} %reshape.83), calls=%async_computation.1 | async-start | bytes 16384 | tf_op jit(solution)/shard_map/all_to_all | solution.py:265
  18.4 2.1 %copy-start.4 = (f32[1088,64,16]{0,1,2:T(8,128)}, f32[1088,64,16]{0,1,2:T(8,128)S(1)}, u32[]{:S(2)}) copy-start(f32[1088,64,16]{0,1,2:T(8,128)S(1)} %convolution_multiply_fusion) | copy-start | bytes 13369348
  20.5 19.3 %copy-start.2 = (bf16[1024,576]{0,1:T(8,128)(2,1)S(1)}, bf16[1024,576]{0,1:T(8,128)(2,1)}, u32[]{:S(2)}) copy-start(bf16[1024,576]{0,1:T(8,128)(2,1)} %param.13) | copy-start | bytes 3538948
  39.9 9.9 %copy-start.1 = (f32[3584]{0:T(1024)S(1)}, f32[3584]{0:T(1024)}, u32[]{:S(2)}) copy-start(f32[3584]{0:T(1024)} %param.18) | copy-start | bytes 43012
  46.2 10.3 %all-to-all-start = ((bf16[64,8,256]{2,0,1:T(8,128)(2,1)}), bf16[64,8,256]{2,0,1:T(8,128)(2,1)S(1)}, u32[]{:S(2)}, u32[]{:S(2)}) async-start(bf16[64,8,256]{2,0,1:T(8,128)(2,1)} %copy.68), calls=%async_computation | async-start | bytes 524288 | tf_op jit(solution)/shard_map/all_to_all | solution.py:282
  120.9 7.5 %copy-start.3 = (bf16[32,16,3584]{2,1,0:T(8,128)(2,1)S(1)}, bf16[32,16,3584]{2,1,0:T(8,128)(2,1)}, u32[]{:S(2)}) copy-start(bf16[32,16,3584]{2,1,0:T(8,128)(2,1)} %get-tuple-element.7) | copy-start | bytes 11010052
Sparse Core Ops, SparseCore 0:
  9.2 30.5 all-gather.1

commit v3 on v2

--- a/solution.py
+++ b/solution.py
@@ -27,7 +27,7 @@
         core + plane + t_bits,
         core + plane[1:] + t_bits + plane[:1],
         core + t_bits + plane,
-    )
+    ) * 2
 
 
 def piece_columns(width, count):
@@ -102,7 +102,7 @@
     count = len(orders)
     held, pending = [], []
     for p in range(count):
-        project(lhs[p], w_ref, bufs[p], columns[p][0])
+        project(lhs[p % len(lhs)], w_ref, bufs[p], columns[p][0])
         copy, low = halve(orders[p], 0, 0, bufs[p], gots[p], send_sem.at[p], recv_sem.at[p])
         pending.append(copy)
         held.append(low)
@@ -132,10 +132,12 @@
         copy.wait_send()
 
 
-def attention_out_kernel(
-    orders, columns, sizes, l0, l1, l2, w_ref, res_ref, gain_ref, hid_ref, all_ref,
-    b0, b1, b2, g0, g1, g2, a0, a1, a2, send_sem, recv_sem, ag_send, ag_recv,
-):
+def attention_out_kernel(orders, columns, sizes, *refs):
+    count = len(orders)
+    lhs, refs = refs[: count // 2], refs[count // 2 :]
+    w_ref, res_ref, gain_ref, mix_ref, hid_ref, all_ref, mix_all_ref = refs[:7]
+    bufs, gots, gathered = (refs[7 + i * count : 7 + (i + 1) * count] for i in range(3))
+    send_sem, recv_sem, ag_send, ag_recv = refs[7 + 3 * count :]
     greet(orders[0])
     bits = len(orders[0])
 
@@ -143,19 +145,21 @@
         cols = pl.ds(*columns[p])
         hid_ref[:, cols] = total + res_ref[:, cols].astype(jnp.float32)
 
-    reduce_scatter(
-        orders, columns, (l0, l1, l2), w_ref, (b0, b1, b2), (g0, g1, g2), send_sem, recv_sem, finish
-    )
+    reduce_scatter(orders, columns, lhs, w_ref, bufs, gots, send_sem, recv_sem, finish)
     rows = hid_ref[...]
     scale = lax.rsqrt(jnp.mean(rows * rows, axis=1, keepdims=True) + EPSILON)
     held, copies = [], []
-    gathered = (a0, a1, a2)
     for p, order in enumerate(orders):
         place = 0
         for stage in order:
             place = place * 2 + my_bit(stage)
         cols = pl.ds(*columns[p])
-        gathered[p][place] = (hid_ref[:, cols] * scale * gain_ref[:, cols]).astype(jnp.bfloat16)
+        wide = columns[p][1]
+        gathered[p][place, :, :wide] = (hid_ref[:, cols] * scale * gain_ref[:, cols]).astype(
+            jnp.bfloat16
+        )
+        if p == count - 1:
+            gathered[p][place, :, wide:] = mix_ref[...]
         held.append(place)
     for step in range(bits):
         for p, order in enumerate(orders):
@@ -182,7 +186,10 @@
             for k, stage in enumerate(order):
                 dim = natural_dim(stage, *sizes)
                 natural = natural + lax.rem(i // (1 << (bits - 1 - k)), 2) * (1 << (bits - 1 - dim))
-            all_ref[natural, :, pl.ds(*columns[p])] = gathered[p][i]
+            wide = columns[p][1]
+            all_ref[natural, :, pl.ds(*columns[p])] = gathered[p][i, :, :wide]
+            if p == count - 1:
+                mix_all_ref[natural] = gathered[p][i, :, wide:]
             return 0
 
         lax.fori_loop(0, 1 << bits, place_block, 0)
@@ -190,30 +197,33 @@
         copy.wait_send()
 
 
-def down_kernel(
-    orders, columns, l0, l1, l2, w_ref, hid_ref, out_ref, b0, b1, b2, g0, g1, g2, send_sem, recv_sem
-):
+def down_kernel(orders, columns, *refs):
+    count = len(orders)
+    lhs, refs = refs[: count // 2], refs[count // 2 :]
+    w_ref, hid_ref, out_ref = refs[:3]
+    bufs, gots = refs[3 : 3 + count], refs[3 + count : 3 + 2 * count]
+    send_sem, recv_sem = refs[3 + 2 * count :]
     greet(orders[0])
 
     def finish(p, total):
         cols = pl.ds(*columns[p])
         out_ref[:, cols] = (hid_ref[:, cols] + total).astype(out_ref.dtype)
 
-    reduce_scatter(
-        orders, columns, (l0, l1, l2), w_ref, (b0, b1, b2), (g0, g1, g2), send_sem, recv_sem, finish
-    )
-
-
-def call(kernel, collective_id, args, outs, blocks, block, columns, gathers, steps, cost):
+    reduce_scatter(orders, columns, lhs, w_ref, bufs, gots, send_sem, recv_sem, finish)
+
+
+def call(kernel, collective_id, args, outs, blocks, block, columns, extra, steps, cost):
     vmem = pl.BlockSpec(memory_space=pltpu.VMEM)
     bufs = [pltpu.VMEM((blocks, block, w), jnp.bfloat16) for _, w in columns]
-    sems = [pltpu.SemaphoreType.DMA((len(columns), steps))] * (4 if gathers else 2)
+    sems = [pltpu.SemaphoreType.DMA((len(columns), steps))] * (4 if extra else 2)
+    wider = [w for _, w in columns[:-1]] + [columns[-1][1] + extra]
+    gathered = [pltpu.VMEM((blocks, block, w), jnp.bfloat16) for w in wider] if extra else []
     return pl.pallas_call(
         kernel,
         out_shape=outs,
         in_specs=[vmem] * len(args),
         out_specs=jax.tree.map(lambda _: vmem, outs),
-        scratch_shapes=bufs * (3 if gathers else 2) + sems,
+        scratch_shapes=bufs * 2 + gathered + sems,
         compiler_params=pltpu.CompilerParams(
             collective_id=collective_id, has_side_effects=True, vmem_limit_bytes=VMEM_BYTES
         ),
@@ -258,28 +268,38 @@
     head_count = queries.shape[1]
     local_experts = w_gate.shape[0]
     experts_all = local_experts * group_count
-    everyone = ("expert", "tensor")
-
-    chosen = expert_ids[:, :, None] == jnp.arange(experts_all, dtype=jnp.int32)
-    mix = jnp.sum(jnp.where(chosen, gate_weights[:, :, None], 0.0), axis=1)
-    mix = lax.all_to_all(
-        mix.reshape(tok_rows, group_count, local_experts),
-        "expert",
-        split_axis=1,
-        concat_axis=0,
-        tiled=True,
-    ).reshape(-1, local_experts)
-
-    uv_rows = lax.all_gather(w_uv, "expert", axis=0, tiled=True)
+
+    block = residual.shape[0]
+    first = lax.axis_index("tensor") * block
+    own_ids = lax.dynamic_slice_in_dim(expert_ids, first, block, 0)
+    own_weights = lax.dynamic_slice_in_dim(gate_weights, first, block, 0)
+    chosen = own_ids[:, :, None] == jnp.arange(experts_all, dtype=jnp.int32)
+    mix = jnp.sum(jnp.where(chosen, own_weights[:, :, None], 0.0), axis=1)
+    high = lax.reduce_precision(mix, 8, 7)
+    extra = -(-2 * experts_all // 128) * 128
+    parts = jnp.concatenate([high, mix - high], axis=1).astype(jnp.bfloat16)
+    parts = jnp.pad(parts, ((0, 0), (0, extra - 2 * experts_all)))
+
     attended = attend(queries, latent_cache, new_latents)
-    head_values = jnp.einsum(
-        "htl,hlv->thv",
-        attended,
-        uv_rows.reshape(head_count, LATENT, VDIM),
-        preferred_element_type=jnp.float32,
-    ).astype(jnp.bfloat16)
-    columns = head_values.reshape(tok_rows, group_count, -1)
-    columns = lax.all_to_all(columns, "expert", split_axis=1, concat_axis=0, tiled=True)
+    if w_uv.shape[0] % LATENT == 0:
+        attended = lax.all_to_all(attended, "expert", split_axis=0, concat_axis=0, tiled=True)
+        own_heads = w_uv.shape[0] // LATENT
+        columns = jnp.einsum(
+            "ghtl,hlv->gthv",
+            attended.reshape(group_count, own_heads, tok_rows, LATENT),
+            w_uv.reshape(own_heads, LATENT, VDIM),
+            preferred_element_type=jnp.float32,
+        ).astype(jnp.bfloat16)
+    else:
+        uv_rows = lax.all_gather(w_uv, "expert", axis=0, tiled=True)
+        head_values = jnp.einsum(
+            "htl,hlv->thv",
+            attended,
+            uv_rows.reshape(head_count, LATENT, VDIM),
+            preferred_element_type=jnp.float32,
+        ).astype(jnp.bfloat16)
+        columns = head_values.reshape(tok_rows, group_count, -1)
+        columns = lax.all_to_all(columns, "expert", split_axis=1, concat_axis=0, tiled=True)
     columns = columns.reshape(group_count * tok_rows, -1)
     tensor_n = lax.axis_size("tensor")
     sizes = (group_count, tensor_n)
@@ -287,26 +307,30 @@
     model_width = residual.shape[1]
     cut = piece_columns(model_width, len(orders))
     blocks = group_count * tensor_n
-    block = residual.shape[0]
     steps = len(orders[0])
     flops = 2 * blocks * block * w_out.size
-    own_hidden, normed = call(
+    own_hidden, normed, mix_all = call(
         functools.partial(attention_out_kernel, orders, cut, sizes),
         0,
-        [in_order(columns, o, *sizes) for o in orders]
-        + [w_out, residual, norm_gain.reshape(1, model_width)],
+        [in_order(columns, o, *sizes) for o in orders[: len(orders) // 2]]
+        + [w_out, residual, norm_gain.reshape(1, model_width), parts],
         (
             jax.ShapeDtypeStruct((block, model_width), jnp.float32),
             jax.ShapeDtypeStruct((blocks, block, model_width), jnp.bfloat16),
+            jax.ShapeDtypeStruct((blocks, block, extra), jnp.bfloat16),
         ),
         blocks,
         block,
         cut,
-        True,
+        extra,
         steps,
         pl.CostEstimate(flops=flops, bytes_accessed=w_out.size * 2, transcendentals=0),
     )
     normed = normed.reshape(blocks * block, model_width)
+    mix_all = mix_all.reshape(blocks * block, extra).astype(jnp.float32)
+    mix_all = mix_all[:, :experts_all] + mix_all[:, experts_all : 2 * experts_all]
+    mine = lax.axis_index("expert") * local_experts
+    mix = lax.dynamic_slice_in_dim(mix_all, mine, local_experts, 1)
 
     gate_part = jnp.einsum("nd,edf->nef", normed, w_gate, preferred_element_type=jnp.float32)
     up_part = jnp.einsum("nd,edf->nef", normed, w_up, preferred_element_type=jnp.float32)
@@ -315,12 +339,12 @@
     return call(
         functools.partial(down_kernel, orders, cut),
         1,
-        [in_order(active, o, *sizes) for o in orders] + [w_down.reshape(-1, model_width), own_hidden],
+        [in_order(active, o, *sizes) for o in orders[: len(orders) // 2]] + [w_down.reshape(-1, model_width), own_hidden],
         jax.ShapeDtypeStruct((block, model_width), jnp.bfloat16),
         blocks,
         block,
         cut,
-        False,
+        0,
         steps,
         pl.CostEstimate(flops=2 * blocks * block * w_down.size, bytes_accessed=w_down.size * 2, transcendentals=0),
     )

time: 190 us -> 157 us (0.83)
  between operations: 13.5 us -> 0.17 us
  waiting for transfers between devices: 23.3 us -> 13.7 us
  Pallas kernels: 102 us -> 94.1 us
  starting transfers between devices: 8.76 us -> 5.17 us
  matrix products: 23.6 us -> 26.2 us
    all_gather x1 -> x0, waiting for transfers between devices: 17.9 us -> none  [per_device(): uv_rows = lax.all_gather(w_uv, 'expert', axis=0, tiled=True)]
    all_to_all x2 -> x1, waiting for transfers between devices: 4.68 us -> 13.7 us  [per_device(): lax.all_to_all(attended, 'expert', split_axis=0, concat_axis=0, tiled=True)]
    pallas_call x2, Pallas kernels: 102 us -> 94.1 us  [call(): pl.pallas_call(kernel, out_shape=outs, in_specs=[vmem] * len(args), out_s...]
    all_to_all x2 -> x1, starting transfers between devices: 8.76 us -> 5.17 us  [per_device(): lax.all_to_all(attended, 'expert', split_axis=0, concat_axis=0, tiled=True)]
    dot_general x1 -> x2, matrix products: 5.29 us -> 7.18 us  [the longest x1 6.75 us: attend(): jnp.einsum('htk,kl->htl', attn_probs, key_rows[:, :LATENT], preferred_ele...]
    unnamed x14 -> x16, local copies, waits for them, and re-layouts: 5.42 us -> 4.99 us
  transfers between devices with their start and end apart: 3 -> 1, of which waited for: 2 -> 1; matrix products, arithmetic and copies ran while one was open for 8% -> 1% of each run, Pallas kernels for 0% -> 0%
where the time goes in v3:
time: 157 us; the launch traced here: 156 us
  Pallas kernels  94.1 us (60%)
  matrix products  26.2 us (17%)
  waiting for transfers between devices  13.7 us (9%)
  local copies, waits for them, and re-layouts  13.6 us (9%)
  starting transfers between devices  5.17 us (3%)
  other arithmetic  3.42 us (2%)
    pallas_call x2, Pallas kernels, call(): pl.pallas_call(kernel, out_shape=outs, in_specs=[vmem] * len(args), out_s...  94.1 us
    all_to_all x1, waiting for transfers between devices, per_device(): lax.all_to_all(attended, 'expert', split_axis=0, concat_axis=0, tiled=True)  13.7 us
    dot_general x1, matrix products, per_device(): jnp.einsum('nd,edf->nef', normed, w_up, preferred_element_type=jnp.float32)  8.22 us
    dot_general x1, matrix products, per_device(): jnp.einsum('nd,edf->nef', normed, w_gate, preferred_element_type=jnp.floa...  7.32 us
    dot_general x1, matrix products, attend(): jnp.einsum('htk,kl->htl', attn_probs, key_rows[:, :LATENT], preferred_ele...  6.75 us
    transpose x6, local copies, waits for them, and re-layouts, in_order(): return split.transpose(dims + [bits, bits + 1]).reshape(rows.shape)  5.42 us
    all_to_all x1, starting transfers between devices, per_device(): lax.all_to_all(attended, 'expert', split_axis=0, concat_axis=0, tiled=True)  5.17 us
    unnamed x16, local copies, waits for them, and re-layouts  4.99 us
  transfers between devices with their start and end apart: 1, of which 1 were waited for; matrix products, arithmetic and copies ran while one was open for 1% of the time, Pallas kernels for 0%

profile of v3, /device:TPU:0, one launch (start us, length us, event | category | flops | bytes accessed | tf_op | source)
XLA Modules:
  0.0 156.4 jit_solution(6718813337749513685)
XLA Ops:
  0.0 0.0 copy-start
  0.1 1.1 copy.39
  1.2 0.2 copy-done
  1.4 3.5 %convolution_multiply_fusion = f32[1088,64,16]{0,1,2:T(8,128)S(1)} fusion(bf16[64,576]{0,1:T(8,128)(2,1)S(1)} %copy.39, bf16[64,16,576]{2,1,0:T(8,128)(2,1)S(1)} %copy-done, bf16[1024,576]{0,1:T(8,128)(2,1)} %param.13), kind=kOutput, calls=%fused_computation.2 | convolution fusion | flops 1287077888 | bytes 6889472 | tf_op jit(solution)/shard_map/thc,kc->htk/dot_general | solution.py:238
  4.9 0.0 copy-start.6
  4.9 2.1 %copy-done.6 = f32[1088,64,16]{0,1,2:T(8,128)} copy-done((f32[1088,64,16]{0,1,2:T(8,128)}, f32[1088,64,16]{0,1,2:T(8,128)S(1)}, u32[]{:S(2)}) %copy-start.6) | copy-done | bytes 4456472
  7.0 1.5 exponential_reduce_fusion
  8.5 0.0 copy-start.2
  8.5 0.0 copy-start.3
  8.5 0.0 copy-start.1
  8.5 0.0 copy-start.4
  8.5 6.7 %fusion.6 = bf16[16,64,512]{2,1,0:T(8,128)(2,1)} fusion(f32[16,64]{1,0:T(8,128)S(1)} %exponential_reduce_fusion, bf16[1024,576]{0,1:T(8,128)(2,1)} %param.13, bf16[64,576]{0,1:T(8,128)(2,1)S(1)} %copy.39, f32[1088,64,16]{0,1,2:T(8,128)} %copy-done.6, pred[64,1088]{1,0:T(8,128)(4,1)S(1)} %iota_compare_fusion), kind=kOutput, calls=%fused_computation.13 | convolution fusion | flops 1148061696 | bytes 6832128 | tf_op jit(solution)/shard_map/htk,kl->htl/dot_general | solution.py:247
  15.2 5.2 %all-to-all-start = ((bf16[16,64,512]{2,1,0:T(8,128)(2,1)}), bf16[16,64,512]{2,1,0:T(8,128)(2,1)S(1)}, u32[]{:S(2)}, u32[]{:S(2)}) async-start(bf16[16,64,512]{2,1,0:T(8,128)(2,1)} %fusion.6), calls=%async_computation | async-start | bytes 2097152 | tf_op jit(solution)/shard_map/all_to_all | solution.py:285
  20.4 0.0 copy-done.2
  20.4 0.1 constant_dynamic-slice_fusion
  20.5 0.1 copy.48
  20.6 0.0 copy-done.3
  20.6 0.1 constant_dynamic-slice_fusion.1
  20.6 0.1 copy.47
  20.7 0.0 copy-done.1
  20.7 0.6 reshape.71.refs_5_
  21.3 0.1 select_reduce_fusion
  21.5 0.7 fusion.19.refs_6_
  22.1 13.7 %all-to-all-done = bf16[16,64,512]{2,1,0:T(8,128)(2,1)S(1)} async-done(((bf16[16,64,512]{2,1,0:T(8,128)(2,1)}), bf16[16,64,512]{2,1,0:T(8,128)(2,1)S(1)}, u32[]{:S(2)}, u32[]{:S(2)}) %all-to-all-start) | async-done | bytes 1048608 | tf_op jit(solution)/shard_map/all_to_all | solution.py:285
  35.8 0.0 copy-done.4
  35.8 0.4 fusion.14
  36.3 0.3 copy.43
  36.6 0.2 reshape_reshape.4
  36.7 0.7 copy.44
  37.5 0.7 copy.45
  38.2 0.7 copy.46
  38.9 59.6 %shard_map.118 = (f32[16,3584]{1,0:T(8,128)}, bf16[32,16,3584]{2,1,0:T(8,128)(2,1)}, bf16[32,16,128]{2,1,0:T(8,128)(2,1)}) custom-call(bf16[512,256]{1,0:T(8,128)(2,1)} %bitcast.59, bf16[512,256]{1,0:T(8,128)(2,1)} %bitcast.60, bf16[512,256]{1,0:T(8,128)(2,1)} %bitcast.61, bf16[256,3584]{1,0:T(8,128)(2,1)} %refs_3_.1, bf16[16,3584]{1,0:T(8,128)(2,1)} %refs_4_.1, ...), custom_call_target="tpu_custom_call" | custom-call | flops 939524096 | bytes 1835008 | tf_op jit(solution)/shard_map/pallas_call | solution.py:221
  98.5 0.9 bitcast_convert_fusion
  99.4 0.1 fusion.25
  99.6 0.2 dynamic-slice_add_fusion
  99.8 0.1 copy.49
  99.9 0.0 copy-start.5
  99.9 8.2 %fusion.26 = f32[512,4,256]{2,0,1:T(8,128)S(1)} fusion(bf16[512,3584,1]{1,0,2:T(8,128)(2,1)} %bitcast.64, bf16[4,3584,256]{2,1,0:T(8,128)(2,1)} %param.22), kind=kOutput, calls=%fused_computation.43 | convolution fusion | flops 3758096384 | bytes 13107200 | tf_op jit(solution)/shard_map/nd,edf->nef/dot_general | solution.py:336
  108.1 0.0 copy-done.5
  108.1 7.3 %multiply_convert_fusion = bf16[512,4,256]{2,0,1:T(8,128)(2,1)S(1)} fusion(f32[512,4,256]{2,0,1:T(8,128)S(1)} %fusion.26, bf16[512,3584,1]{1,0,2:T(8,128)(2,1)S(1)} %bitcast.65, bf16[4,3584,256]{2,1,0:T(8,128)(2,1)} %param.21, f32[512,4]{0,1:T(4,128)S(1)} %copy.49), kind=kOutput, calls=%fused_computation.10 | convolution fusion | flops 3761766400 | bytes 14163968 | tf_op jit(solution)/shard_map/nd,edf->nef/dot_general | solution.py:335
  115.5 0.8 copy.50
  116.3 0.8 reshape_reshape.5
  117.0 1.1 copy.51
  118.1 1.1 copy.52
  119.2 1.1 copy.53
  120.3 34.6 %shard_map.119 = bf16[16,3584]{1,0:T(8,128)(2,1)} custom-call(bf16[512,1024]{1,0:T(8,128)(2,1)} %bitcast.56, bf16[512,1024]{1,0:T(8,128)(2,1)} %bitcast.57, bf16[512,1024]{1,0:T(8,128)(2,1)} %bitcast.58, bf16[1024,3584]{1,0:T(8,128)(2,1)} %bitcast.62, f32[16,3584]{1,0:T(8,128)} %get-tuple-element.10.refs_4_), custom_call_target="tpu_custom_call" | custom-call | flops 3758096384 | bytes 7340032 | tf_op jit(solution)/shard_map/pallas_call | solution.py:221
  154.9 1.6 copy.62
  (3 shorter events, 0.1 us)
Async XLA Ops:
  0.0 1.4 copy-start
  4.9 2.1 %copy-start.6 = (f32[1088,64,16]{0,1,2:T(8,128)}, f32[1088,64,16]{0,1,2:T(8,128)S(1)}, u32[]{:S(2)}) copy-start(f32[1088,64,16]{0,1,2:T(8,128)S(1)} %convolution_multiply_fusion) | copy-start | bytes 13369348
  8.5 12.0 %copy-start.2 = (f32[64,8]{0,1:T(8,128)S(1)}, f32[64,8]{0,1:T(8,128)}, u32[]{:S(2)}) copy-start(f32[64,8]{0,1:T(8,128)} %param.20) | copy-start | bytes 6148
  8.5 12.1 %copy-start.3 = (s32[64,8]{0,1:T(8,128)S(1)}, s32[64,8]{0,1:T(8,128)}, u32[]{:S(2)}) copy-start(s32[64,8]{0,1:T(8,128)} %param.19) | copy-start | bytes 6148
  8.5 12.2 %copy-start.1 = (f32[3584]{0:T(1024)S(1)}, f32[3584]{0:T(1024)}, u32[]{:S(2)}) copy-start(f32[3584]{0:T(1024)} %param.18) | copy-start | bytes 43012
  8.5 27.3 %copy-start.4 = (bf16[1024,128]{1,0:T(8,128)(2,1)S(1)}, bf16[1024,128]{1,0:T(8,128)(2,1)}, u32[]{:S(2)}) copy-start(bf16[1024,128]{1,0:T(8,128)(2,1)} %param.16) | copy-start | bytes 786436
  15.2 20.6 %all-to-all-start = ((bf16[16,64,512]{2,1,0:T(8,128)(2,1)}), bf16[16,64,512]{2,1,0:T(8,128)(2,1)S(1)}, u32[]{:S(2)}, u32[]{:S(2)}) async-start(bf16[16,64,512]{2,1,0:T(8,128)(2,1)} %fusion.6), calls=%async_computation | async-start | bytes 2097152 | tf_op jit(solution)/shard_map/all_to_all | solution.py:285
  99.9 8.2 %copy-start.5 = (bf16[32,16,3584]{2,1,0:T(8,128)(2,1)S(1)}, bf16[32,16,3584]{2,1,0:T(8,128)(2,1)}, u32[]{:S(2)}) copy-start(bf16[32,16,3584]{2,1,0:T(8,128)(2,1)} %get-tuple-element.8) | copy-start | bytes 11010052

commit v4 on v3

--- a/solution.py
+++ b/solution.py
@@ -210,6 +210,79 @@
         out_ref[:, cols] = (hid_ref[:, cols] + total).astype(out_ref.dtype)
 
     reduce_scatter(orders, columns, lhs, w_ref, bufs, gots, send_sem, recv_sem, finish)
+
+
+def experts_kernel(orders, columns, sizes, *refs):
+    x_ref, mix_ref, gate_hbm, up_hbm, down_hbm, hid_ref, out_ref = refs[:7]
+    count = len(orders)
+    refs = refs[7:]
+    bufs, gots, lhs = refs[:count], refs[count : 2 * count], refs[2 * count : 2 * count + count // 2]
+    gate_ref, up_ref, down_ref, send_sem, recv_sem, load_sem = refs[2 * count + count // 2 :]
+    experts, _, hidden_units = gate_ref.shape
+
+    def load(e):
+        return (
+            pltpu.make_async_copy(gate_hbm.at[e], gate_ref.at[e], load_sem.at[0, e]),
+            pltpu.make_async_copy(up_hbm.at[e], up_ref.at[e], load_sem.at[1, e]),
+        )
+
+    for e in range(experts):
+        for copy in load(e):
+            copy.start()
+    load_down = pltpu.make_async_copy(down_hbm, down_ref, load_sem.at[2, 0])
+    load_down.start()
+    greet(orders[0])
+    bits = len(orders[0])
+    block = hid_ref.shape[0]
+
+    def one_expert(e, _):
+        for copy in load(e):
+            copy.wait()
+        gate = jnp.dot(x_ref[...], gate_ref[e], preferred_element_type=jnp.float32)
+        up = jnp.dot(x_ref[...], up_ref[e], preferred_element_type=jnp.float32)
+        active = (gate / (1.0 + jnp.exp(-gate)) * up * mix_ref[e]).astype(jnp.bfloat16)
+        cols = pl.ds(pl.multiple_of(e * hidden_units, hidden_units), hidden_units)
+        for order, rows_ref in zip(orders, lhs):
+            dims = [natural_dim(stage, *sizes) for stage in order]
+            for i in range(1 << bits):
+                natural = sum((i >> (bits - 1 - k) & 1) << (bits - 1 - d) for k, d in enumerate(dims))
+                rows_ref[pl.ds(i * block, block), cols] = active[natural * block : (natural + 1) * block]
+        return 0
+
+    lax.fori_loop(0, experts, one_expert, 0)
+    load_down.wait()
+
+    def finish(p, total):
+        cols = pl.ds(*columns[p])
+        out_ref[:, cols] = (hid_ref[:, cols] + total).astype(out_ref.dtype)
+
+    reduce_scatter(orders, columns, lhs, down_ref, bufs, gots, send_sem, recv_sem, finish)
+
+
+def call_experts(orders, columns, sizes, normed, mix, w_gate, w_up, w_down, own_hidden):
+    vmem, anywhere = pl.BlockSpec(memory_space=pltpu.VMEM), pl.BlockSpec(memory_space=pl.ANY)
+    block, model_width = own_hidden.shape
+    rows = normed.shape[0]
+    bufs = [pltpu.VMEM((rows // block, block, w), jnp.bfloat16) for _, w in columns]
+    lhs = [pltpu.VMEM((rows, w_down.shape[0]), jnp.bfloat16)] * (len(orders) // 2)
+    sems = [pltpu.SemaphoreType.DMA((len(columns), len(orders[0])))] * 2
+    return pl.pallas_call(
+        functools.partial(experts_kernel, orders, columns, sizes),
+        out_shape=jax.ShapeDtypeStruct((block, model_width), jnp.bfloat16),
+        in_specs=[vmem, vmem, anywhere, anywhere, anywhere, vmem],
+        out_specs=vmem,
+        scratch_shapes=bufs * 2
+        + lhs
+        + [pltpu.VMEM(w.shape, jnp.bfloat16) for w in (w_gate, w_up, w_down)]
+        + sems
+        + [pltpu.SemaphoreType.DMA((3, w_gate.shape[0]))],
+        compiler_params=pltpu.CompilerParams(
+            collective_id=2, has_side_effects=True, vmem_limit_bytes=VMEM_BYTES
+        ),
+        cost_estimate=pl.CostEstimate(
+            flops=6 * rows * w_down.size, bytes_accessed=6 * w_down.size, transcendentals=0
+        ),
+    )(normed, mix.T[:, :, None], w_gate, w_up, w_down, own_hidden)
 
 
 def call(kernel, collective_id, args, outs, blocks, block, columns, extra, steps, cost):
@@ -332,6 +405,11 @@
     mine = lax.axis_index("expert") * local_experts
     mix = lax.dynamic_slice_in_dim(mix_all, mine, local_experts, 1)
 
+    held_bytes = 2 * (3 * w_down.size + 3 * normed.size + 3 * normed.shape[0] * w_down.size // model_width)
+    if held_bytes < VMEM_BYTES * 3 // 4:
+        down_rows = w_down.reshape(-1, model_width)
+        return call_experts(orders, cut, sizes, normed, mix, w_gate, w_up, down_rows, own_hidden)
+
     gate_part = jnp.einsum("nd,edf->nef", normed, w_gate, preferred_element_type=jnp.float32)
     up_part = jnp.einsum("nd,edf->nef", normed, w_up, preferred_element_type=jnp.float32)
     active = (jax.nn.silu(gate_part) * up_part * mix[:, :, None]).astype(jnp.bfloat16)

time: 157 us -> 148 us (0.943)
  matrix products: 26.2 us -> 10.7 us
  Pallas kernels: 94.1 us -> 102 us
    pallas_call x0 -> x1, Pallas kernels: none -> 42.3 us  [call_experts(): pl.pallas_call(functools.partial(experts_kernel, orders, columns, sizes),...]
    pallas_call x2 -> x1, Pallas kernels: 94.1 us -> 59.5 us  [call(): pl.pallas_call(kernel, out_shape=outs, in_specs=[vmem] * len(args), out_s...]
    dot_general x2 -> x0, matrix products: 15.5 us -> none  [the longest x1 8.22 us: per_device(): jnp.einsum('nd,edf->nef', normed, w_up, preferred_element_type=jnp.float32)]
    broadcast_in_dim x0 -> x1, local copies, waits for them, and re-layouts: none -> 4.64 us  [call_experts(): mix.T[:, :, None]]
    transpose x6 -> x3, local copies, waits for them, and re-layouts: 5.42 us -> 2.18 us  [in_order(): return split.transpose(dims + [bits, bits + 1]).reshape(rows.shape)]
    unnamed x16 -> x14, local copies, waits for them, and re-layouts: 4.99 us -> 4.98 us
where the time goes in v4:
time: 148 us
  Pallas kernels  102 us (69%)
  waiting for transfers between devices  13.7 us (9%)
  local copies, waits for them, and re-layouts  13.3 us (9%)
  matrix products  10.7 us (7%)
  starting transfers between devices  5.17 us (3%)
  other arithmetic  3.43 us (2%)
    pallas_call x1, Pallas kernels, call(): pl.pallas_call(kernel, out_shape=outs, in_specs=[vmem] * len(args), out_s...  59.5 us
    pallas_call x1, Pallas kernels, call_experts(): pl.pallas_call(functools.partial(experts_kernel, orders, columns, sizes),...  42.3 us
    all_to_all x1, waiting for transfers between devices, per_device(): lax.all_to_all(attended, 'expert', split_axis=0, concat_axis=0, tiled=True)  13.7 us
    dot_general x1, matrix products, attend(): jnp.einsum('htk,kl->htl', attn_probs, key_rows[:, :LATENT], preferred_ele...  6.75 us
    all_to_all x1, starting transfers between devices, per_device(): lax.all_to_all(attended, 'expert', split_axis=0, concat_axis=0, tiled=True)  5.17 us
    unnamed x14, local copies, waits for them, and re-layouts  4.98 us
    broadcast_in_dim x1, local copies, waits for them, and re-layouts, call_experts(): mix.T[:, :, None]  4.64 us
    dot_general x1, matrix products, attend(): jnp.einsum('thc,kc->htk', queries, key_rows, preferred_element_type=jnp.f...  3.51 us
  transfers between devices with their start and end apart: 1, of which 1 were waited for; matrix products, arithmetic and copies ran while one was open for 1% of the time, Pallas kernels for 0%

profile of v4, /device:TPU:0, one launch (start us, length us, event | category | flops | bytes accessed | tf_op | source)
XLA Modules:
  0.0 148.1 jit_solution(16421926615235559540)
XLA Ops:
  0.0 0.0 copy-start
  0.0 1.1 copy.34
  1.2 0.2 copy-done
  1.4 3.5 %convolution_multiply_fusion = f32[1088,64,16]{0,1,2:T(8,128)S(1)} fusion(bf16[64,576]{0,1:T(8,128)(2,1)S(1)} %copy.34, bf16[64,16,576]{2,1,0:T(8,128)(2,1)S(1)} %copy-done, bf16[1024,576]{0,1:T(8,128)(2,1)} %param.13), kind=kOutput, calls=%fused_computation.2 | convolution fusion | flops 1287077888 | bytes 6889472 | tf_op jit(solution)/shard_map/thc,kc->htk/dot_general | solution.py:311
  4.9 0.0 copy-start.5
  4.9 2.1 %copy-done.5 = f32[1088,64,16]{0,1,2:T(8,128)} copy-done((f32[1088,64,16]{0,1,2:T(8,128)}, f32[1088,64,16]{0,1,2:T(8,128)S(1)}, u32[]{:S(2)}) %copy-start.5) | copy-done | bytes 4456472
  7.0 1.5 exponential_reduce_fusion
  8.5 0.0 copy-start.1
  8.5 0.0 copy-start.2
  8.5 0.0 copy-start.3
  8.5 0.0 copy-start.4
  8.5 6.7 %fusion.6 = bf16[16,64,512]{2,1,0:T(8,128)(2,1)} fusion(f32[16,64]{1,0:T(8,128)S(1)} %exponential_reduce_fusion, bf16[1024,576]{0,1:T(8,128)(2,1)} %param.13, bf16[64,576]{0,1:T(8,128)(2,1)S(1)} %copy.34, f32[1088,64,16]{0,1,2:T(8,128)} %copy-done.5, pred[64,1088]{1,0:T(8,128)(4,1)S(1)} %iota_compare_fusion), kind=kOutput, calls=%fused_computation.12 | convolution fusion | flops 1148061696 | bytes 6832128 | tf_op jit(solution)/shard_map/htk,kl->htl/dot_general | solution.py:320
  15.3 5.2 %all-to-all-start = ((bf16[16,64,512]{2,1,0:T(8,128)(2,1)}), bf16[16,64,512]{2,1,0:T(8,128)(2,1)S(1)}, u32[]{:S(2)}, u32[]{:S(2)}) async-start(bf16[16,64,512]{2,1,0:T(8,128)(2,1)} %fusion.6), calls=%async_computation | async-start | bytes 2097152 | tf_op jit(solution)/shard_map/all_to_all | solution.py:358
  20.4 0.0 copy-done.1
  20.4 0.6 reshape.61.refs_5_
  21.0 0.0 copy-done.2
  21.0 0.1 constant_dynamic-slice_fusion
  21.1 0.1 copy.43
  21.2 0.0 copy-done.3
  21.2 0.1 constant_dynamic-slice_fusion.1
  21.3 0.1 copy.42
  21.3 0.1 select_reduce_fusion
  21.5 0.7 fusion.20.refs_6_
  22.1 13.7 %all-to-all-done = bf16[16,64,512]{2,1,0:T(8,128)(2,1)S(1)} async-done(((bf16[16,64,512]{2,1,0:T(8,128)(2,1)}), bf16[16,64,512]{2,1,0:T(8,128)(2,1)S(1)}, u32[]{:S(2)}, u32[]{:S(2)}) %all-to-all-start) | async-done | bytes 1048608 | tf_op jit(solution)/shard_map/all_to_all | solution.py:358
  35.8 0.0 copy-done.4
  35.8 0.4 fusion.14
  36.3 0.3 copy.38
  36.6 0.2 reshape_reshape.2
  36.7 0.7 copy.39
  37.5 0.7 copy.40
  38.2 0.7 copy.41
  38.9 59.5 %shard_map.118 = (f32[16,3584]{1,0:T(8,128)}, bf16[32,16,3584]{2,1,0:T(8,128)(2,1)}, bf16[32,16,128]{2,1,0:T(8,128)(2,1)}) custom-call(bf16[512,256]{1,0:T(8,128)(2,1)} %bitcast.45, bf16[512,256]{1,0:T(8,128)(2,1)} %bitcast.46, bf16[512,256]{1,0:T(8,128)(2,1)} %bitcast.47, bf16[256,3584]{1,0:T(8,128)(2,1)} %refs_3_.2, bf16[16,3584]{1,0:T(8,128)(2,1)} %refs_4_.1, ...), custom_call_target="tpu_custom_call" | custom-call | flops 939524096 | bytes 1835008 | tf_op jit(solution)/shard_map/pallas_call | solution.py:294
  98.4 0.9 bitcast_convert_fusion
  99.3 0.1 fusion.26
  99.5 0.2 fusion.16
  99.7 4.6 %copy.45.refs_1_ = f32[4,512,1]{2,1,0:T(8,128)} copy(f32[4,512,1]{0,1,2:T(8,128)S(1)} %fusion.16) | data formatting | bytes 16384 | tf_op jit(solution)/shard_map/broadcast_in_dim | solution.py:285
  104.3 42.3 %shard_map.119 = bf16[16,3584]{1,0:T(8,128)(2,1)} custom-call(bf16[512,3584]{1,0:T(8,128)(2,1)} %bitcast.50, f32[4,512,1]{2,1,0:T(8,128)} %copy.45.refs_1_, bf16[4,3584,256]{2,1,0:T(8,128)(2,1)} %refs_2_.1, bf16[4,3584,256]{2,1,0:T(8,128)(2,1)} %refs_3_.3, bf16[1024,3584]{1,0:T(8,128)(2,1)} %bitcast.48, f32[16,3584]{1,0:T(8,128)} %get-tuple-element.10.refs_5_), custom_call_target="tpu_custom_call" | custom-call | flops 11274289152 | bytes 22020096 | tf_op jit(solution)/shard_map/pallas_call | solution.py:269
  146.6 1.6 %copy.56 = bf16[16,3584]{1,0:T(8,128)(2,1)} copy(bf16[16,3584]{1,0:T(8,128)(2,1)} %shard_map.119) | data formatting | bytes 229376
  (3 shorter events, 0.1 us)
Async XLA Ops:
  0.0 1.4 copy-start
  4.9 2.1 %copy-start.5 = (f32[1088,64,16]{0,1,2:T(8,128)}, f32[1088,64,16]{0,1,2:T(8,128)S(1)}, u32[]{:S(2)}) copy-start(f32[1088,64,16]{0,1,2:T(8,128)S(1)} %convolution_multiply_fusion) | copy-start | bytes 13369348
  8.5 12.0 %copy-start.1 = (f32[3584]{0:T(1024)S(1)}, f32[3584]{0:T(1024)}, u32[]{:S(2)}) copy-start(f32[3584]{0:T(1024)} %param.18) | copy-start | bytes 43012
  8.5 12.6 %copy-start.2 = (f32[64,8]{0,1:T(8,128)S(1)}, f32[64,8]{0,1:T(8,128)}, u32[]{:S(2)}) copy-start(f32[64,8]{0,1:T(8,128)} %param.20) | copy-start | bytes 6148
  8.5 12.7 %copy-start.3 = (s32[64,8]{0,1:T(8,128)S(1)}, s32[64,8]{0,1:T(8,128)}, u32[]{:S(2)}) copy-start(s32[64,8]{0,1:T(8,128)} %param.19) | copy-start | bytes 6148
  8.5 27.3 %copy-start.4 = (bf16[1024,128]{1,0:T(8,128)(2,1)S(1)}, bf16[1024,128]{1,0:T(8,128)(2,1)}, u32[]{:S(2)}) copy-start(bf16[1024,128]{1,0:T(8,128)(2,1)} %param.16) | copy-start | bytes 786436
  15.3 20.6 %all-to-all-start = ((bf16[16,64,512]{2,1,0:T(8,128)(2,1)}), bf16[16,64,512]{2,1,0:T(8,128)(2,1)S(1)}, u32[]{:S(2)}, u32[]{:S(2)}) async-start(bf16[16,64,512]{2,1,0:T(8,128)(2,1)} %fusion.6), calls=%async_computation | async-start | bytes 2097152 | tf_op jit(solution)/shard_map/all_to_all | solution.py:358
